TPU v7x, 32 devices: a whole 2x2x4 slice. The times are simulated.
32 devices in a mesh: task: 4 (over y, x), feat: 8 (over z, core).
Axes of the slice: x: 2, y: 2, z: 4, core: 2. Of those that a mesh axis runs over, the one named last changes fastest.
Arguments:
- layer_input: bfloat16 [8, 16, 512, 512], P('task', 'feat'), may hold values from -6 to 6
- cotangent: bfloat16 [8, 16, 512, 512], P('task', 'feat'), may hold values from -6 to 6
- sample_len: int32 [8], P('task'), may hold values from 50 to 512, as said below
- feat_count: int32 [8], P('task'), may hold values from 4 to 16, as said below
- ln1_gain: float32 [512], replicated, may hold values from 0.5 to 1.5
- ln1_bias: float32 [512], replicated, may hold values from -2 to 2
- qkv1_weight: bfloat16 [512, 1536], replicated, may hold values from -0.375 to 0.375
- out1_weight: bfloat16 [512, 512], replicated, may hold values from -1 to 1
- ln2_gain: float32 [512], replicated, may hold values from 0.5 to 1.5
- ln2_bias: float32 [512], replicated, may hold values from -2 to 2
- qkv2_weight: bfloat16 [512, 1536], replicated, may hold values from -0.375 to 0.375
- out2_weight: bfloat16 [512, 512], replicated, may hold values from -0.75 to 0.75
- ln3_gain: float32 [512], replicated, may hold values from 0.5 to 1.5
- ln3_bias: float32 [512], replicated, may hold values from -2 to 2
- up_weight: bfloat16 [512, 2048], replicated, may hold values from -0.25 to 0.25
- up_bias: float32 [2048], replicated, may hold values from -3 to 3
- down_weight: bfloat16 [2048, 512], replicated, may hold values from -0.125 to 0.125
- down_bias: float32 [512], replicated, may hold values from -3 to 3
Outputs:
- layer_output: bfloat16 [8, 16, 512, 512], P('task', 'feat')
- input_grad: bfloat16 [8, 16, 512, 512], P('task', 'feat')
- ln1_gain_grad: float32 [512], P('feat')
- ln1_bias_grad: float32 [512], P('feat')
- qkv1_weight_grad: float32 [512, 1536], P('feat')
- out1_weight_grad: float32 [512, 512], P('feat')
- ln2_gain_grad: float32 [512], P('feat')
- ln2_bias_grad: float32 [512], P('feat')
- qkv2_weight_grad: float32 [512, 1536], P('feat')
- out2_weight_grad: float32 [512, 512], P('feat')
- ln3_gain_grad: float32 [512], P('feat')
- ln3_bias_grad: float32 [512], P('feat')
- up_weight_grad: float32 [512, 2048], P('feat')
- up_bias_grad: float32 [2048], P('feat')
- down_weight_grad: float32 [2048, 512], P('feat')
- down_bias_grad: float32 [512], P('feat')
Inputs may be any that keep to these rules, and one draw needn't show every extreme that they name: `sample_len`: in every block of 2 consecutive tasks one task has all 512 samples. `feat_count`: in every block of 2 consecutive tasks one task has all 16 features.
All inputs are finite; a program needn't handle non-finite values.
Results may differ from a plain program's by a relative error of at most 0.024.
Values may be sent and summed in bfloat16 or wider, within the bound.
No kernel may reach another device: no remote copies, remote signals or barrier semaphores. Data moves between devices by JAX's collectives and lax.ppermute only.
A program may use at most 256 MiB of HBM per device.

v0:
```python
from functools import partial

import jax
import jax.numpy as jnp
from jax import lax
from jax.sharding import PartitionSpec as P

HEADS = 8
HEAD_DIM = 64


EPSILON = 1e-05


def normalize(hidden, factor, offset):
    average = jnp.mean(hidden, axis=-1, keepdims=True)
    centred = hidden - average
    variance = jnp.mean(centred * centred, axis=-1, keepdims=True)
    return centred * lax.rsqrt(variance + EPSILON) * factor + offset


def project(left, matrix):
    return jnp.einsum("tfsd,de->tfse", left, matrix, preferred_element_type=jnp.float32)


def back_project(left, matrix):
    return jnp.einsum("tfse,de->tfsd", left, matrix, preferred_element_type=jnp.float32)


def outer_sum(left, right):
    return jnp.einsum("tfsd,tfse->de", left, right, preferred_element_type=jnp.float32)


def split_packed(packed):
    pieces = packed.reshape(packed.shape[:-1] + (3, HEADS, HEAD_DIM))
    return (pieces[..., 0, :, :], pieces[..., 1, :, :], pieces[..., 2, :, :])


def score_rows(queries, keys_all, key_mask, layout):
    key_layout = layout.replace("q", "k")
    scaling = queries.shape[-1] ** (-0.5)
    scores = (
        jnp.einsum(
            layout + "," + key_layout + "->tfhqk",
            queries,
            keys_all,
            preferred_element_type=jnp.float32,
        )
        * scaling
    )
    return jnp.where(key_mask, scores, -1e30)


def attend(packed, key_mask, layout):
    queries, keys_all, values_all = split_packed(packed)
    key_layout = layout.replace("q", "k")
    scores = score_rows(queries, keys_all, key_mask, layout)
    row_max = jnp.max(scores, axis=-1, keepdims=True)
    exp_terms = jnp.exp(scores - row_max)
    totals = jnp.sum(exp_terms, axis=-1, keepdims=True)
    weights = (exp_terms / totals).astype(jnp.bfloat16)
    head_rows = jnp.einsum(
        "tfhqk," + key_layout + "->" + layout,
        weights,
        values_all,
        preferred_element_type=jnp.float32,
    ).astype(jnp.bfloat16)
    return (head_rows.reshape(head_rows.shape[:-2] + (-1,)), row_max + jnp.log(totals))


def attend_back(packed, key_mask, log_totals, grad_heads, layout):
    queries, keys_all, values_all = split_packed(packed)
    key_layout = layout.replace("q", "k")
    scaling = queries.shape[-1] ** (-0.5)
    grad_output = grad_heads.reshape(grad_heads.shape[:-1] + (HEADS, HEAD_DIM))
    scores = score_rows(queries, keys_all, key_mask, layout)
    probabilities = jnp.exp(scores - log_totals)
    grad_probs = jnp.einsum(
        layout + "," + key_layout + "->tfhqk",
        grad_output,
        values_all,
        preferred_element_type=jnp.float32,
    )
    row_dot = jnp.sum(probabilities * grad_probs, axis=-1, keepdims=True)
    grad_scores = (probabilities * (grad_probs - row_dot)).astype(jnp.bfloat16)
    grad_queries = (
        jnp.einsum(
            "tfhqk," + key_layout + "->" + layout,
            grad_scores,
            keys_all,
            preferred_element_type=jnp.float32,
        )
        * scaling
    )
    grad_keys = (
        jnp.einsum(
            "tfhqk," + layout + "->" + key_layout,
            grad_scores,
            queries,
            preferred_element_type=jnp.float32,
        )
        * scaling
    )
    grad_values = jnp.einsum(
        "tfhqk," + layout + "->" + key_layout,
        probabilities.astype(jnp.bfloat16),
        grad_output,
        preferred_element_type=jnp.float32,
    )
    stacked = jnp.stack([grad_queries, grad_keys, grad_values], axis=-3)
    return stacked.reshape(stacked.shape[:-3] + (-1,)).astype(jnp.bfloat16)


def body(
    layer_input,
    cotangent,
    sample_len,
    feat_count,
    ln1_gain,
    ln1_bias,
    qkv1_weight,
    out1_weight,
    ln2_gain,
    ln2_bias,
    qkv2_weight,
    out2_weight,
    ln3_gain,
    ln3_bias,
    up_weight,
    up_bias,
    down_weight,
    down_bias,
):
    tasks_here, feats_here, samples, feature_width = layer_input.shape
    feats_all = feats_here * lax.axis_size("feat")
    sample_keep = (jnp.arange(samples)[None, :] < sample_len[:, None]).reshape(
        tasks_here, 1, 1, 1, samples
    )
    feat_keep = (jnp.arange(feats_all)[None, :] < feat_count[:, None]).reshape(
        tasks_here, 1, 1, 1, feats_all
    )
    inputs = layer_input.astype(jnp.float32)
    normed_one = normalize(inputs, ln1_gain, ln1_bias).astype(jnp.bfloat16)
    packed_one = project(normed_one, qkv1_weight).astype(jnp.bfloat16)
    heads_one, log_one = attend(packed_one, sample_keep, "tfqhe")
    middle_one = inputs + project(heads_one, out1_weight)
    normed_two = normalize(middle_one, ln2_gain, ln2_bias).astype(jnp.bfloat16)
    packed_two = lax.all_to_all(
        project(normed_two, qkv2_weight).astype(jnp.bfloat16),
        "feat",
        split_axis=2,
        concat_axis=1,
        tiled=True,
    )
    heads_moved, log_two = attend(packed_two, feat_keep, "tqfhe")
    heads_two = lax.all_to_all(heads_moved, "feat", split_axis=1, concat_axis=2, tiled=True)
    middle_two = middle_one + project(heads_two, out2_weight)
    normed_three = normalize(middle_two, ln3_gain, ln3_bias).astype(jnp.bfloat16)
    preact = project(normed_three, up_weight) + up_bias
    activated = jax.nn.gelu(preact, approximate=False).astype(jnp.bfloat16)
    result = middle_two + project(activated, down_weight) + down_bias
    upstream = cotangent.astype(jnp.float32)
    down_grad = outer_sum(activated, cotangent)
    down_shift_grad = jnp.sum(cotangent, axis=(0, 1, 2), dtype=jnp.float32)
    _, gelu_pullback = jax.vjp(partial(jax.nn.gelu, approximate=False), preact)
    grad_preact = gelu_pullback(back_project(cotangent, down_weight))[0].astype(jnp.bfloat16)
    up_grad = outer_sum(normed_three, grad_preact)
    up_shift_grad = jnp.sum(grad_preact, axis=(0, 1, 2), dtype=jnp.float32)
    _, norm_pullback = jax.vjp(normalize, middle_two, ln3_gain, ln3_bias)
    from_norm, gain_three_grad, shift_three_grad = norm_pullback(
        back_project(grad_preact, up_weight)
    )
    grad_middle_two = upstream + from_norm
    rounded_two = grad_middle_two.astype(jnp.bfloat16)
    project_two_grad = outer_sum(heads_two, rounded_two)
    grad_heads_two = back_project(rounded_two, out2_weight).astype(jnp.bfloat16)
    grad_heads_moved = lax.all_to_all(
        grad_heads_two, "feat", split_axis=2, concat_axis=1, tiled=True
    )
    grad_packed_two = attend_back(packed_two, feat_keep, log_two, grad_heads_moved, "tqfhe")
    grad_packed_local = lax.all_to_all(
        grad_packed_two, "feat", split_axis=1, concat_axis=2, tiled=True
    )
    packed_two_grad = outer_sum(normed_two, grad_packed_local)
    grad_normed_two = back_project(grad_packed_local, qkv2_weight).astype(jnp.bfloat16)
    _, norm_pullback = jax.vjp(normalize, middle_one, ln2_gain, ln2_bias)
    from_norm, gain_two_grad, shift_two_grad = norm_pullback(grad_normed_two.astype(jnp.float32))
    grad_middle_one = grad_middle_two + from_norm
    rounded_one = grad_middle_one.astype(jnp.bfloat16)
    project_one_grad = outer_sum(heads_one, rounded_one)
    grad_heads_one = back_project(rounded_one, out1_weight).astype(jnp.bfloat16)
    grad_packed_one = attend_back(packed_one, sample_keep, log_one, grad_heads_one, "tfqhe")
    packed_one_grad = outer_sum(normed_one, grad_packed_one)
    grad_normed_one = back_project(grad_packed_one, qkv1_weight)
    _, norm_pullback = jax.vjp(normalize, inputs, ln1_gain, ln1_bias)
    from_norm, gain_one_grad, shift_one_grad = norm_pullback(grad_normed_one)
    grad_inputs = (grad_middle_one + from_norm).astype(jnp.bfloat16)
    shards = (
        lax.psum_scatter(gain_one_grad, "feat", scatter_dimension=0, tiled=True),
        lax.psum_scatter(shift_one_grad, "feat", scatter_dimension=0, tiled=True),
        lax.psum_scatter(packed_one_grad, "feat", scatter_dimension=0, tiled=True),
        lax.psum_scatter(project_one_grad, "feat", scatter_dimension=0, tiled=True),
        lax.psum_scatter(gain_two_grad, "feat", scatter_dimension=0, tiled=True),
        lax.psum_scatter(shift_two_grad, "feat", scatter_dimension=0, tiled=True),
        lax.psum_scatter(packed_two_grad, "feat", scatter_dimension=0, tiled=True),
        lax.psum_scatter(project_two_grad, "feat", scatter_dimension=0, tiled=True),
        lax.psum_scatter(gain_three_grad, "feat", scatter_dimension=0, tiled=True),
        lax.psum_scatter(shift_three_grad, "feat", scatter_dimension=0, tiled=True),
        lax.psum_scatter(up_grad, "feat", scatter_dimension=0, tiled=True),
        lax.psum_scatter(up_shift_grad, "feat", scatter_dimension=0, tiled=True),
        lax.psum_scatter(down_grad, "feat", scatter_dimension=0, tiled=True),
        lax.psum_scatter(down_shift_grad, "feat", scatter_dimension=0, tiled=True),
    )
    totals = (
        lax.psum(shards[0].astype(jnp.bfloat16), "task").astype(jnp.float32),
        lax.psum(shards[1].astype(jnp.bfloat16), "task").astype(jnp.float32),
        lax.psum(shards[2].astype(jnp.bfloat16), "task").astype(jnp.float32),
        lax.psum(shards[3].astype(jnp.bfloat16), "task").astype(jnp.float32),
        lax.psum(shards[4].astype(jnp.bfloat16), "task").astype(jnp.float32),
        lax.psum(shards[5].astype(jnp.bfloat16), "task").astype(jnp.float32),
        lax.psum(shards[6].astype(jnp.bfloat16), "task").astype(jnp.float32),
        lax.psum(shards[7].astype(jnp.bfloat16), "task").astype(jnp.float32),
        lax.psum(shards[8].astype(jnp.bfloat16), "task").astype(jnp.float32),
        lax.psum(shards[9].astype(jnp.bfloat16), "task").astype(jnp.float32),
        lax.psum(shards[10].astype(jnp.bfloat16), "task").astype(jnp.float32),
        lax.psum(shards[11].astype(jnp.bfloat16), "task").astype(jnp.float32),
        lax.psum(shards[12].astype(jnp.bfloat16), "task").astype(jnp.float32),
        lax.psum(shards[13].astype(jnp.bfloat16), "task").astype(jnp.float32),
    )
    return (
        result.astype(jnp.bfloat16),
        grad_inputs,
        totals[0],
        totals[1],
        totals[2],
        totals[3],
        totals[4],
        totals[5],
        totals[6],
        totals[7],
        totals[8],
        totals[9],
        totals[10],
        totals[11],
        totals[12],
        totals[13],
    )


def solution(mesh):
    return jax.shard_map(
        body,
        mesh=mesh,
        in_specs=(
            P("task", "feat", None, None),
            P("task", "feat", None, None),
            P("task"),
            P("task"),
            P(),
            P(),
            P(),
            P(),
            P(),
            P(),
            P(),
            P(),
            P(),
            P(),
            P(),
            P(),
            P(),
            P(),
        ),
        out_specs=(
            P("task", "feat", None, None),
            P("task", "feat", None, None),
            P("feat"),
            P("feat"),
            P("feat", None),
            P("feat", None),
            P("feat"),
            P("feat"),
            P("feat", None),
            P("feat", None),
            P("feat"),
            P("feat"),
            P("feat", None),
            P("feat"),
            P("feat", None),
            P("feat"),
        ),
        check_vma=False,
    )
```

profile of v0, /device:TPU:0, one launch (start us, length us, event | category | flops | bytes accessed | tf_op | source)
XLA Modules:
  0.0 1085.7 jit_solution(11403357615835268526)
XLA Ops:
  17.0 5.8 convolution_convert_fusion.1
  22.7 8.6 copy.128
  31.4 16.7 %fusion.12 = (f32[2,2,8,512]{3,2,1,0:T(8,128)S(1)}, f32[2,2,8,512,512]{3,4,2,1,0:T(8,128)}) fusion(pred[2,512]{1,0:T(4,128)(4,1)S(1)} %iota_compare_fusion, bf16[2,2,512,3,8,64]{2,5,4,3,1,0:T(8,128)(2,1)} %bitcast.215), kind=kOutput, calls=%fused_computation.33 | convolution fusion | flops 1098891264 | bytes 37815296 | tf_op jit(solution)/shard_map/tfqhe,tfkhe->tfhqk/dot_general | solution.py:43
  48.1 14.6 %fusion = f32[2,2,8,512]{3,2,1,0:T(8,128)S(1)} fusion(f32[2,2,8,512]{3,2,1,0:T(8,128)S(1)} %get-tuple-element.106, f32[2,2,8,512,512]{3,4,2,1,0:T(8,128)} %get-tuple-element.107, pred[2,512]{1,0:T(4,128)(4,1)S(1)} %iota_compare_fusion), kind=kLoop, calls=%fused_computation.6 | loop fusion | flops 33538048 | bytes 33686528 | tf_op jit(solution)/shard_map/reduce_sum | solution.py:60
  62.7 16.9 %fusion.87 = bf16[2,2,8,64,512]{4,3,2,1,0:T(8,128)(2,1)} fusion(f32[2,2,8,512]{3,2,1,0:T(8,128)S(1)} %fusion, f32[2,2,8,512]{3,2,1,0:T(8,128)S(1)} %get-tuple-element.106, f32[2,2,8,512,512]{3,4,2,1,0:T(8,128)} %get-tuple-element.107, pred[2,512]{1,0:T(4,128)(4,1)S(1)} %iota_compare_fusion, bf16[2,2,512,3,8,64]{2,5,4,3,1,0:T(8,128)(2,1)} %bitcast.216), kind=kOutput, calls=%fused_computation.141 | convolution fusion | flops 1116733440 | bytes 37880832 | tf_op jit(solution)/shard_map/tfhqk,tfkhe->tfqhe/dot_general | solution.py:62
  90.3 27.2 %copy.136 = bf16[2,2,512,1536]{3,1,0,2:T(2,128)(2,1)} copy(bf16[2,2,512,1536]{3,2,1,0:T(8,128)(2,1)S(1)} %convolution_convert_fusion) | data formatting | bytes 12582912 | tf_op jit(solution)/shard_map/convert_element_type | solution.py:149
  117.5 6.7 all-to-all-start
  124.3 138.9 %all-to-all-done = bf16[2,2,512,1536]{3,1,0,2:T(2,128)(2,1)} async-done(((bf16[2,2,512,1536]{3,1,0,2:T(2,128)(2,1)}), bf16[2,2,512,1536]{3,1,0,2:T(2,128)(2,1)}, u32[]{:S(2)}, u32[]{:S(2)}) %all-to-all-start) | async-done | bytes 6291488 | tf_op jit(solution)/shard_map/all_to_all | solution.py:148
  263.2 6.9 copy.309
  270.1 16.2 %reshape.216 = bf16[2,16,64,3,8,64]{5,4,3,2,1,0:T(8,128)(2,1)} reshape(bf16[2,8,2,64,1536]{4,3,2,1,0:T(8,128)(2,1)} %bitcast.220) | data formatting | bytes 12582912 | tf_op jit(solution)/shard_map/reshape | solution.py:35
  286.3 8.9 fusion.131
  295.1 9.8 fusion.52
  310.3 6.1 convert_bitcast_fusion.1
  316.5 5.2 copy.220
  321.7 6.5 reshape.234
  336.7 44.9 %all-to-all-done.1 = bf16[2,16,64,512]{3,2,0,1:T(8,128)(2,1)} async-done(((bf16[2,16,64,512]{3,2,0,1:T(8,128)(2,1)}), bf16[2,16,64,512]{3,2,0,1:T(8,128)(2,1)}, u32[]{:S(2)}, u32[]{:S(2)}) %all-to-all-start.1) | async-done | bytes 2097184 | tf_op jit(solution)/shard_map/all_to_all | solution.py:156
  387.7 16.6 %fusion.45 = (u8[2,512,2048]{2,1,0:T(8,128)(4,1)}, u8[2,512,2048]{2,1,0:T(8,128)(4,1)}, f32[2,2,512,2048]{3,2,1,0:T(8,128)}) fusion(f32[2048]{0:T(1024)S(1)} %copy-done.52, bf16[512,2048]{1,0:T(8,128)(2,1)S(1)} %copy-done, f32[2,2,512,512]{2,3,1,0:T(8,128)S(1)} %get-tuple-element.113, f32[512]{0:T(512)S(1)} %copy-done.63, f32[512]{0:T(512)S(1)} %copy-done.57, ...), kind=kOutput, calls=%fused_computation.105 | convolution fusion | flops 4354736128 | bytes 27291648 | tf_op jit(solution)/shard_map/tfsd,de->tfse/dot_general | solution.py:23
  404.4 42.3 %multiply_convert_fusion.1 = (bf16[2,2,512,2048]{3,2,1,0:T(8,128)(2,1)}, f32[2,2,512,2048]{3,2,1,0:T(8,128)}) fusion(f32[2,2,512,2048]{3,2,1,0:T(8,128)} %get-tuple-element.114, f32[2048]{0:T(1024)S(1)} %copy-done.52, u8[2,512,2048]{2,1,0:T(8,128)(4,1)} %get-tuple-element.65, u8[2,512,2048]{2,1,0:T(8,128)(4,1)} %get-tuple-element.64), kind=kLoop, calls=%fused_computation.19 | loop fusion | flops 297795584 | bytes 46145536 | tf_op jit(solution)/shard_map/convert_element_type | solution.py:160
  446.6 22.3 %convert_reduce_fusion = (f32[2048]{0:T(1024)}, bf16[2,2,512,2048]{3,2,1,0:T(8,128)(2,1)}) fusion(f32[2,2,512,2048]{3,2,1,0:T(8,128)} %get-tuple-element.101, bf16[2,2,512,512]{3,2,1,0:T(8,128)(2,1)} %param.19, bf16[2048,512]{1,0:T(8,128)(2,1)} %param.34, f32[2,2,512,2048]{3,2,1,0:T(8,128)} %get-tuple-element.114, f32[2048]{0:T(1024)S(1)} %copy-done.52), kind=kOutput, calls=%fused_computation.16 | convolution fusion | flops 4366268416 | bytes 46153728 | tf_op jit(solution)/shard_map/tfse,de->tfsd/dot_general | solution.py:27
  468.9 10.2 fusion.135
  479.1 5.4 copy.150
  484.5 5.5 multiply_reduce_fusion.2
  510.1 11.2 %fusion.59 = f32[512,2048]{1,0:T(8,128)} fusion(bf16[2,2,512,2048]{3,2,1,0:T(8,128)(2,1)} %get-tuple-element.125, f32[2,2,512,512]{2,3,1,0:T(8,128)} %copy-done.9, f32[512]{0:T(512)S(1)} %copy-done.63, f32[512]{0:T(512)S(1)} %copy-done.57, f32[2,2,512]{2,1,0:T(2,128)S(1)} %fusion.119, f32[2,2,512]{2,1,0:T(2,128)S(1)} %broadcast_multiply_fusion), kind=kOutput, calls=%fused_computation.115 | convolution fusion | flops 4300210176 | bytes 16797696 | tf_op jit(solution)/shard_map/tfsd,tfse->de/dot_general | solution.py:31
  521.3 41.8 %all-to-all-done.2 = bf16[2,2,512,512]{3,1,0,2:T(2,128)(2,1)} async-done(((bf16[2,2,512,512]{3,1,0,2:T(2,128)(2,1)}), bf16[2,2,512,512]{3,1,0,2:T(2,128)(2,1)}, u32[]{:S(2)}, u32[]{:S(2)}) %all-to-all-start.2) | async-done | bytes 2097184 | tf_op jit(solution)/shard_map/all_to_all | solution.py:177
  566.6 6.4 reshape.218
  573.0 16.4 %multiply_reduce_fusion.1 = (f32[2,64,8,16]{3,2,1,0:T(8,128)S(1)}, f32[2,64,8,16,16]{3,4,2,1,0:T(8,128)}) fusion(f32[2,64,8,16]{3,2,1,0:T(8,128)S(1)} %log_add_fusion, f32[2,64,8,16,16]{3,4,2,1,0:T(8,128)} %copy-done.2, pred[2,16]{1,0:T(4,128)(4,1)S(1)} %iota_compare_fusion.1, bf16[2,16,64,1,8,64]{5,4,3,2,1,0:T(8,128)(2,1)} %get-tuple-element.102, ...), kind=kOutput, calls=%fused_computation.42 | convolution fusion | flops 34848768 | bytes 6422560 | tf_op jit(solution)/shard_map/tqfhe,tkfhe->tfhqk/dot_general | solution.py:78
  589.4 7.6 multiply_convert_fusion.4
  597.0 4.8 fusion.40
  601.9 5.0 fusion.41
  606.9 9.6 convert_bitcast_fusion
  616.5 7.3 pad_maximum_fusion
  623.8 8.6 copy.223
  632.4 16.8 %reshape.235 = bf16[2,16,64,1536]{3,2,0,1:T(8,128)(2,1)} reshape(bf16[2,16,64,3,8,64]{5,4,3,2,0,1:T(8,128)(2,1)} %copy.223) | data formatting | bytes 12582912 | tf_op jit(solution)/shard_map/convert_element_type | solution.py:111
  654.2 10.5 fusion.62
  664.8 167.5 %all-to-all-done.3 = bf16[2,16,64,1536]{3,2,0,1:T(8,128)(2,1)} async-done(((bf16[2,16,64,1536]{3,2,0,1:T(8,128)(2,1)}), bf16[2,16,64,1536]{3,2,0,1:T(8,128)(2,1)}, u32[]{:S(2)}, u32[]{:S(2)}) %all-to-all-start.3) | async-done | bytes 6291488 | tf_op jit(solution)/shard_map/all_to_all | solution.py:181
  854.2 8.7 fusion.53
  863.0 25.3 %multiply_reduce_fusion = (f32[2,2,8,512]{3,2,1,0:T(8,128)S(1)}, f32[2,2,8,512,512]{3,4,2,1,0:T(8,128)}) fusion(f32[2,2,8,512]{3,2,1,0:T(8,128)S(1)} %log_add_fusion.1, f32[2,2,8,512,512]{3,4,2,1,0:T(8,128)} %get-tuple-element.107, pred[2,512]{1,0:T(4,128)(4,1)S(1)} %copy-done.37, bf16[2,2,512,8,64]{2,4,3,1,0:T(8,128)(2,1)S(1)} %bitcast.230, ...), kind=kOutput, calls=%fused_computation.1 | convolution fusion | flops 1115668480 | bytes 71435264 | tf_op jit(solution)/shard_map/tfqhe,tfkhe->tfhqk/dot_general | solution.py:78
  888.3 28.3 %multiply_convert_fusion = bf16[2,2,8,512,512]{3,4,2,1,0:T(8,128)(2,1)} fusion(f32[2,2,8,512,512]{3,4,2,1,0:T(8,128)} %get-tuple-element.119, f32[2,2,8,512]{3,2,1,0:T(8,128)S(1)} %get-tuple-element.118, f32[2,2,8,512]{3,2,1,0:T(8,128)S(1)} %log_add_fusion.1, f32[2,2,8,512,512]{3,4,2,1,0:T(8,128)} %get-tuple-element.107, pred[2,512]{1,0:T(4,128)(4,1)S(1)} %copy-done.37), kind=kLoop, calls=%fused_computation | loop fusion | flops 50331648 | bytes 84018176 | tf_op jit(solution)/shard_map/convert_element_type | solution.py:85
  916.7 9.4 fusion.94
  926.0 12.9 %fusion.95 = bf16[2,2,512,1,8,64]{2,5,4,1,0,3:T(8,128)(2,1)} fusion(bf16[2,2,8,512,512]{3,4,2,1,0:T(8,128)(2,1)} %multiply_convert_fusion, bf16[2,2,512,3,8,64]{2,5,4,3,1,0:T(8,128)(2,1)} %bitcast.219), kind=kOutput, calls=%fused_computation.148 | convolution fusion | flops 1075838976 | bytes 20971520 | tf_op jit(solution)/shard_map/tfhqk,tfqhe->tfkhe/dot_general | solution.py:96
  938.9 16.5 %convert_bitcast_fusion.2 = bf16[2,2,512,1,8,64]{2,5,4,1,0,3:T(8,128)(2,1)} fusion(bf16[2,2,512,8,64]{2,4,3,1,0:T(8,128)(2,1)} %bitcast.231, f32[2,2,8,512]{3,2,1,0:T(8,128)S(1)} %log_add_fusion.1, f32[2,2,8,512,512]{3,4,2,1,0:T(8,128)} %get-tuple-element.107, pred[2,512]{1,0:T(4,128)(4,1)S(1)} %copy-done.37), kind=kOutput, calls=%fused_computation.140 | convolution fusion | flops 1108344832 | bytes 37815296 | tf_op jit(solution)/shard_map/tfhqk,tfqhe->tfkhe/dot_general | solution.py:104
  961.9 5.1 fusion.56
  969.0 11.6 %add_convert_fusion.2 = bf16[2,2,512,512]{2,3,1,0:T(8,128)(2,1)} fusion(f32[2,2,512,512]{2,3,1,0:T(8,128)} %copy-done.9, f32[512]{0:T(512)S(1)} %copy-done.68, bf16[2,2,512,2048]{3,2,1,0:T(8,128)(2,1)} %get-tuple-element.100, bf16[2048,512]{1,0:T(8,128)(2,1)} %param.34), kind=kOutput, calls=%fused_computation.97 | convolution fusion | flops 4298113024 | bytes 16779264 | tf_op jit(solution)/shard_map/tfsd,de->tfse/dot_general | solution.py:23
  990.1 8.8 fusion.134
  998.9 5.3 copy.168
  1016.2 26.6 %all-reduce.8 = (bf16[512]{0:T(512)(128)(2,1)S(1)}, bf16[512]{0:T(512)(128)(2,1)S(1)}, bf16[512]{0:T(512)(128)(2,1)S(1)}, bf16[512]{0:T(512)(128)(2,1)S(1)}, bf1...) all-reduce(f32[512]{0:T(512)S(1)} %get-tuple-element.70, ...), channel_id=2, replica_groups=mesh['task'=4,'feat'=8] {'feat'}, use_global_device_ids=true, to_apply=%region_19.20.clone | all-reduce | flops 5632 | bytes 33792
  1043.4 9.9 all-reduce.9
  1057.4 7.1 add_convert_fusion.1
  (240 shorter events, 137.8 us)
Async XLA Ops:
  7.2 380.4 %copy-start = (bf16[512,2048]{1,0:T(8,128)(2,1)S(1)}, bf16[512,2048]{1,0:T(8,128)(2,1)}, u32[]{:S(2)}) copy-start(bf16[512,2048]{1,0:T(8,128)(2,1)} %param.32) | copy-start | bytes 6291460
  7.2 9.8 copy-start.50
  7.2 9.7 copy-start.66
  11.5 5.5 copy-start.7
  11.5 5.5 copy-start.62
  22.7 8.6 copy-start.59
  31.4 31.2 %copy-start.36 = (pred[2,512]{1,0:T(4,128)(4,1)}, pred[2,512]{1,0:T(4,128)(4,1)S(1)}, u32[]{:S(2)}) copy-start(pred[2,512]{1,0:T(4,128)(4,1)S(1)} %iota_compare_fusion) | copy-start | bytes 3076
  48.1 14.6 %copy-start.29 = (f32[2,2,8,512]{3,2,1,0:T(8,128)}, f32[2,2,8,512]{3,2,1,0:T(8,128)S(1)}, u32[]{:S(2)}) copy-start(f32[2,2,8,512]{3,2,1,0:T(8,128)S(1)} %get-tuple-element.106) | copy-start | bytes 196612
  62.7 16.9 %copy-start.34 = (f32[2,2,8,512]{3,2,1,0:T(8,128)}, f32[2,2,8,512]{3,2,1,0:T(8,128)S(1)}, u32[]{:S(2)}) copy-start(f32[2,2,8,512]{3,2,1,0:T(8,128)S(1)} %fusion) | copy-start | bytes 196612
  62.7 16.9 %copy-start.32 = (bf16[512,512]{1,0:T(8,128)(2,1)S(1)}, bf16[512,512]{1,0:T(8,128)(2,1)}, u32[]{:S(2)}) copy-start(bf16[512,512]{1,0:T(8,128)(2,1)} %param.25) | copy-start | bytes 1572868
  83.4 6.9 copy-start.3
  83.5 6.8 copy-start.40
  86.1 4.2 copy-start.42
  117.5 6.7 copy-start.69
  117.5 145.7 %all-to-all-start = ((bf16[2,2,512,1536]{3,1,0,2:T(2,128)(2,1)}), bf16[2,2,512,1536]{3,1,0,2:T(2,128)(2,1)}, u32[]{:S(2)}, u32[]{:S(2)}) async-start(bf16[2,2,512,1536]{3,1,0,2:T(2,128)(2,1)} %copy.136), calls=%async_computation | async-start | bytes 12582912 | tf_op jit(solution)/shard_map/all_to_all | solution.py:148
  304.9 4.3 copy-start.2
  305.0 4.5 copy-start.26
  305.0 5.4 copy-start.18
  308.2 8.2 copy-start.28
  328.2 53.4 %all-to-all-start.1 = ((bf16[2,16,64,512]{3,2,0,1:T(8,128)(2,1)}), bf16[2,16,64,512]{3,2,0,1:T(8,128)(2,1)}, u32[]{:S(2)}, u32[]{:S(2)}) async-start(bf16[2,16,64,512]{3,2,0,1:T(8,128)(2,1)} %reshape.234), calls=%async_computation.1 | async-start | bytes 4194304 | tf_op jit(solution)/shard_map/all_to_all | solution.py:156
  386.9 17.4 %copy-start.9 = (f32[2,2,512,512]{2,3,1,0:T(8,128)}, f32[2,2,512,512]{2,3,1,0:T(8,128)S(1)}, u32[]{:S(2)}) copy-start(f32[2,2,512,512]{2,3,1,0:T(8,128)S(1)} %get-tuple-element.113) | copy-start | bytes 12582916
  484.5 5.6 copy-start.10
  484.5 5.9 copy-start.14
  499.9 63.3 %all-to-all-start.2 = ((bf16[2,2,512,512]{3,1,0,2:T(2,128)(2,1)}), bf16[2,2,512,512]{3,1,0,2:T(2,128)(2,1)}, u32[]{:S(2)}, u32[]{:S(2)}) async-start(bf16[2,2,512,512]{3,1,0,2:T(2,128)(2,1)} %copy.152), calls=%async_computation.2 | async-start | bytes 4194304 | tf_op jit(solution)/shard_map/all_to_all | solution.py:177
  504.3 4.7 copy-start.27
  504.3 480.7 %reduce-scatter.13.cloned.1.call-start = ((), (), s32[]{:S(2)}) async-start(), calls=%async_computation.13 | async-start | bytes 1179648 | tf_op jit(solution)/shard_map/reduce_scatter | solution.py:206
  508.9 477.6 %reduce-scatter.15.cloned.1.call-start = ((), (), s32[]{:S(2)}) async-start(), calls=%async_computation.14 | async-start | bytes 4718592 | tf_op jit(solution)/shard_map/reduce_scatter | solution.py:209
  589.4 7.6 copy-start.17
  597.0 4.9 copy-start.16
  601.9 5.0 copy-start.11
  649.3 183.0 %all-to-all-start.3 = ((bf16[2,16,64,1536]{3,2,0,1:T(8,128)(2,1)}), bf16[2,16,64,1536]{3,2,0,1:T(8,128)(2,1)}, u32[]{:S(2)}, u32[]{:S(2)}) async-start(bf16[2,16,64,1536]{3,2,0,1:T(8,128)(2,1)} %reshape.235), calls=%async_computation.3 | async-start | bytes 12582912 | tf_op jit(solution)/shard_map/all_to_all | solution.py:181
  654.0 334.3 %reduce-scatter.17.cloned.1.call-start = ((), (), s32[]{:S(2)}) async-start(), calls=%async_computation.15 | async-start | bytes 4718592 | tf_op jit(solution)/shard_map/reduce_scatter | solution.py:211
  664.7 342.5 %reduce-scatter.9.cloned.1.call-start = ((), (), s32[]{:S(2)}) async-start(), calls=%async_computation.11 | async-start | bytes 1179648 | tf_op jit(solution)/shard_map/reduce_scatter | solution.py:202
  832.3 4.5 copy-start.61
  835.9 4.9 copy-start.21
  836.8 4.0 copy-start.43
  843.0 5.5 copy-start.22
  850.8 158.0 %reduce-scatter.11.cloned.1.call-start = ((), (), s32[]{:S(2)}) async-start(), calls=%async_computation.12 | async-start | bytes 3538944 | tf_op jit(solution)/shard_map/reduce_scatter | solution.py:205
  854.2 8.8 copy-start.23
  854.2 8.8 copy-start.37
  863.0 147.6 %reduce-scatter.7.cloned.1.call-start = ((), (), s32[]{:S(2)}) async-start(), calls=%async_computation.10 | async-start | bytes 3538944 | tf_op jit(solution)/shard_map/reduce_scatter | solution.py:201
  961.9 5.2 copy-start.70
  961.9 7.1 copy-start.68
  967.1 101.6 %all-reduce.13.cloned.1.call-start = ((), (), s32[]{:S(2)}) async-start(), calls=%async_computation.16 | async-start | bytes 2097152 | tf_op jit(solution)/shard_map/psum | solution.py:217
  1008.8 7.3 copy-start.55
  1008.8 7.3 copy-start.56
  1008.8 7.3 copy-start.58
  1057.4 21.3 %copy-start.1 = (bf16[512,2048]{1,0:T(8,128)(2,1)S(1)}, bf16[512,2048]{1,0:T(8,128)(2,1)}, u32[]{:S(2)}) copy-start(bf16[512,2048]{1,0:T(8,128)(2,1)} %param.32) | copy-start | bytes 6291460
  (34 other events, 84.4 us)
Sparse Core Ops, SparseCore 0:
  509.0 39.3 reduce-scatter.12
  550.7 59.0 reduce-scatter.14
  664.8 113.5 reduce-scatter.16
  851.0 31.1 reduce-scatter.8
  884.3 38.7 reduce-scatter.10
  967.2 39.5 reduce-scatter.6
  1012.4 52.5 all-reduce.12
where the time goes:
time: 1100 us; the launch traced here: 1090 us
  waiting for transfers between devices  393 us (36%)
  matrix products  286 us (26%)
  local copies, waits for them, and re-layouts  168 us (15%)
  other arithmetic  165 us (15%)
  blocking collectives  36.5 us (3%)
  starting transfers between devices  20.8 us (2%)
  between operations  16.6 us (2%)
    all_to_all x1, waiting for transfers between devices, body(): lax.all_to_all(grad_packed_two, 'feat', split_axis=1, concat_axis=2, tile...  168 us
    all_to_all x1, waiting for transfers between devices, body(): lax.all_to_all(project(normed_two, qkv2_weight).astype(jnp.bfloat16), 'fe...  139 us
    dot_general x6, matrix products, back_project(): jnp.einsum('tfse,de->tfsd', left, matrix, preferred_element_type=jnp.floa...  49.6 us
    all_to_all x1, waiting for transfers between devices, body(): lax.all_to_all(heads_moved, 'feat', split_axis=1, concat_axis=2, tiled=True)  44.9 us
    dot_general x6, matrix products, project(): jnp.einsum('tfsd,de->tfse', left, matrix, preferred_element_type=jnp.floa...  44.6 us
    dot_general x6, matrix products, outer_sum(): jnp.einsum('tfsd,tfse->de', left, right, preferred_element_type=jnp.float32)  42.3 us
    convert_element_type x1, other arithmetic, body(): activated = jax.nn.gelu(preact, approximate=False).astype(jnp.bfloat16)  42.3 us
    all_to_all x1, waiting for transfers between devices, body(): lax.all_to_all(grad_heads_two, 'feat', split_axis=2, concat_axis=1, tiled...  41.8 us
  transfers between devices with their start and end apart: 11, of which 4 were waited for; matrix products, arithmetic and copies ran while one was open for 28% of the time, Pallas kernels for 0%

commit v1 on v0

v1 whole, which is shorter than its diff:
```python
import math
from functools import partial
import jax, jax.numpy as jnp
from jax import lax
from jax.experimental import pallas as pl
from jax.experimental.pallas import tpu as pltpu
BF=jnp.bfloat16; F32=jnp.float32
EPS=1e-5
LOG2E=1.4426950408889634
QS=0.125*LOG2E

def dg(a,b,ca,cb):
    return lax.dot_general(a,b,(((ca,),(cb,)),((),())),preferred_element_type=F32)

def ln_stats(v):
    mean=jnp.mean(v,axis=-1,keepdims=True)
    c=v-mean
    var=jnp.mean(c*c,axis=-1,keepdims=True)
    return c, lax.rsqrt(var+EPS)

def split3(v):
    a=v.astype(BF); r=v-a.astype(F32)
    b=r.astype(BF); r=r-b.astype(F32)
    return a,b,r.astype(BF)

def pad_head(rows,u,aug):
    z=jnp.zeros_like(rows)
    return jnp.concatenate([rows,z,aug] if u==0 else [z,rows,aug],axis=0)

def lane_block(cols,n):
    lane=lax.broadcasted_iota(jnp.int32,(n,128),1)
    out=jnp.zeros((n,128),F32)
    for i,c in enumerate(cols):
        out=jnp.where(lane==i,c,out)
    return out.astype(BF)

def row_block(rows,n):
    sub=lax.broadcasted_iota(jnp.int32,(128,n),0)
    out=jnp.zeros((128,n),F32)
    for i,r in enumerate(rows):
        out=jnp.where(sub==i,r,out)
    return out.astype(BF)

def a_kernel(t, len_ref, x_ref, g_ref, b_ref, w_ref, wo_ref, mid_ref, qt_ref, k_ref, v_ref, ht_ref, l_ref):
    S,D=x_ref.shape[2:]
    x=x_ref[0,0].astype(F32)
    c,r=ln_stats(x)
    n1=(c*r*g_ref[...]+b_ref[...]).astype(BF)
    qt_ref[0]=(dg(w_ref[:,0:D],n1,0,1)*QS).astype(BF)
    k_ref[0]=dg(n1,w_ref[:,D:2*D],1,0).astype(BF)
    v_ref[0]=dg(n1,w_ref[:,2*D:3*D],1,0).astype(BF)
    n=len_ref[t]
    ks=lax.broadcasted_iota(jnp.int32,(S,1),0)
    bias=jnp.where(ks<n,0.0,-1e30)
    kb=lane_block([bias],S)
    qa=row_block([jnp.ones((1,S),F32)],S)
    ones=jnp.ones((16,S),BF)
    for p in range(D//128):
        kp=jnp.concatenate([k_ref[0,:,p*128:p*128+128],kb],axis=1)
        vt=v_ref[0,:,p*128:p*128+128].T
        for u in range(2):
            h=2*p+u
            q=pad_head(qt_ref[0,h*64:h*64+64,:],u,qa)
            s=dg(kp,q,1,0)
            m=jnp.max(s,axis=0,keepdims=True)
            e=jnp.exp2(s-m).astype(BF)
            va=jnp.concatenate([vt[u*64:u*64+64],ones],axis=0)
            o=dg(va,e,1,0)
            l=o[64:65]
            ht_ref[0,h*64:h*64+64,:]=(o[:64]*(1.0/l)).astype(BF)
            l_ref[0,h:h+1,:]=m+jnp.log2(l)
    mid=(x+dg(ht_ref[0],wo_ref[...],0,0)).astype(BF)
    nd=mid_ref.shape[0]
    for j in range(nd):
        mid_ref[j,0]=mid[j*(S//nd):(j+1)*(S//nd)]

def run_a(t, lens, x, g, b, w, wo, nd):
    T,F,S,D=x.shape
    grid_spec=pltpu.PrefetchScalarGridSpec(num_scalar_prefetch=1,grid=(F,),
        in_specs=[pl.BlockSpec((1,1,S,D),lambda f,s:(t,f,0,0)),
                  pl.BlockSpec((1,D),lambda f,s:(0,0)),pl.BlockSpec((1,D),lambda f,s:(0,0)),
                  pl.BlockSpec((D,3*D),lambda f,s:(0,0)),pl.BlockSpec((D,D),lambda f,s:(0,0))],
        out_specs=[pl.BlockSpec((nd,1,S//nd,D),lambda f,s:(0,f,0,0)),
                   pl.BlockSpec((1,D,S),lambda f,s:(f,0,0)),
                   pl.BlockSpec((1,S,D),lambda f,s:(f,0,0)),
                   pl.BlockSpec((1,S,D),lambda f,s:(f,0,0)),
                   pl.BlockSpec((1,D,S),lambda f,s:(f,0,0)),
                   pl.BlockSpec((1,D//64,S),lambda f,s:(f,0,0))])
    sd=jax.ShapeDtypeStruct
    return pl.pallas_call(partial(a_kernel,t),grid_spec=grid_spec,
        out_shape=[sd((nd,F,S//nd,D),BF),sd((F,D,S),BF),sd((F,S,D),BF),sd((F,S,D),BF),sd((F,D,S),BF),sd((F,D//64,S),F32)],
        compiler_params=pltpu.CompilerParams(vmem_limit_bytes=60<<20),name="fwd_samples",
        cost_estimate=pl.CostEstimate(flops=20_000_000_000,bytes_accessed=8<<20,transcendentals=4<<20))(lens,x,g.reshape(1,D),b.reshape(1,D),w,wo)

LN2=0.6931471805599453

def c_kernel(t, len_ref, x_ref, gm_ref, g_ref, b_ref, w_ref, wo_ref, qt_ref, k_ref, v_ref, ht_ref, l_ref, dx_ref, dw_ref, dwo_ref, dgb_ref, dot_ref, dpt_ref):
    S,D=x_ref.shape[2:]
    f=pl.program_id(0)
    x=x_ref[0,0].astype(F32)
    c,r=ln_stats(x)
    xh=c*r
    n1=(xh*g_ref[...]+b_ref[...]).astype(BF)
    nd=gm_ref.shape[0]
    s_in=jnp.concatenate([gm_ref[j,0] for j in range(nd)],axis=0)
    dot_ref[...]=dg(wo_ref[...],s_in,1,1).astype(BF)
    n=len_ref[t]
    ks=lax.broadcasted_iota(jnp.int32,(S,1),0)
    bias=jnp.where(ks<n,0.0,-1e30)
    one=jnp.ones((S,1),F32)
    kb=lane_block([bias,one,one,one],S)
    vb=lane_block([one,one,one],S)
    oner=jnp.ones((1,S),F32)
    for p in range(D//128):
        kp=jnp.concatenate([k_ref[0,:,p*128:p*128+128],kb],axis=1)
        vp=jnp.concatenate([v_ref[0,:,p*128:p*128+128],vb],axis=1)
        kt=k_ref[0,:,p*128:p*128+128].T
        for u in range(2):
            h=2*p+u
            hs=slice(h*64,h*64+64)
            L=l_ref[0,h:h+1,:]
            do=dot_ref[hs,:]
            dd=jnp.sum(do.astype(F32)*ht_ref[0,hs,:].astype(F32),axis=0,keepdims=True)
            l3=[-z.astype(F32) for z in split3(L)]
            d3=[-z.astype(F32) for z in split3(dd)]
            qa=row_block([oner]+l3,S)
            da=row_block(d3,S)
            s=dg(kp,pad_head(qt_ref[0,hs,:],u,qa),1,0)
            e=jnp.exp2(s)
            dp=dg(vp,pad_head(do,u,da),1,0)
            ds=(e*dp).astype(BF)
            e=e.astype(BF)
            dpt_ref[2*D+h*64:2*D+h*64+64,:]=dg(do,e,1,1).astype(BF)
            dpt_ref[D+h*64:D+h*64+64,:]=(dg(qt_ref[0,hs,:],ds,1,1)*LN2).astype(BF)
            dpt_ref[h*64:h*64+64,:]=(dg(kt[u*64:u*64+64],ds,1,0)*0.125).astype(BF)
    dw=dg(n1,dpt_ref[...],0,1)
    dwo=dg(ht_ref[0],s_in,1,0)
    dn=dg(dpt_ref[...],w_ref[...],0,1)
    dgain=jnp.sum(dn*xh,axis=0,keepdims=True)
    dbias=jnp.sum(dn,axis=0,keepdims=True)
    gd=dn*g_ref[...]
    dv=r*(gd-jnp.mean(gd,axis=-1,keepdims=True)-xh*jnp.mean(gd*xh,axis=-1,keepdims=True))
    dx_ref[0]=(s_in.astype(F32)+dv).astype(BF)
    @pl.when(f==0)
    def _():
        dw_ref[...]=dw; dwo_ref[...]=dwo
        dgb_ref[0:1]=dgain; dgb_ref[1:2]=dbias
    @pl.when(f>0)
    def _():
        dw_ref[...]+=dw; dwo_ref[...]+=dwo
        dgb_ref[0:1]+=dgain; dgb_ref[1:2]+=dbias

def run_c(t, lens, x, gm, g, b, w, wo, qt, k, v, ht, l):
    T,F,S,D=x.shape; nd=gm.shape[0]
    gs=pltpu.PrefetchScalarGridSpec(num_scalar_prefetch=1,grid=(F,),
        in_specs=[pl.BlockSpec((1,1,S,D),lambda f,s:(t,f,0,0)),
                  pl.BlockSpec((nd,1,S//nd,D),lambda f,s:(0,f,0,0)),
                  pl.BlockSpec((1,D),lambda f,s:(0,0)),pl.BlockSpec((1,D),lambda f,s:(0,0)),
                  pl.BlockSpec((D,3*D),lambda f,s:(0,0)),pl.BlockSpec((D,D),lambda f,s:(0,0)),
                   pl.BlockSpec((1,D,S),lambda f,s:(f,0,0)),
                   pl.BlockSpec((1,S,D),lambda f,s:(f,0,0)),
                   pl.BlockSpec((1,S,D),lambda f,s:(f,0,0)),
                   pl.BlockSpec((1,D,S),lambda f,s:(f,0,0)),
                   pl.BlockSpec((1,D//64,S),lambda f,s:(f,0,0))],
        out_specs=[pl.BlockSpec((1,S,D),lambda f,s:(f,0,0)),
                   pl.BlockSpec((D,3*D),lambda f,s:(0,0)),pl.BlockSpec((D,D),lambda f,s:(0,0)),
                   pl.BlockSpec((8,D),lambda f,s:(0,0))],
        scratch_shapes=[pltpu.VMEM((D,S),BF),pltpu.VMEM((3*D,S),BF)])
    sd=jax.ShapeDtypeStruct
    return pl.pallas_call(partial(c_kernel,t),grid_spec=gs,
        out_shape=[sd((F,S,D),BF),sd((D,3*D),F32),sd((D,D),F32),sd((8,D),F32)],
        compiler_params=pltpu.CompilerParams(vmem_limit_bytes=60<<20),name="bwd_samples",
        cost_estimate=pl.CostEstimate(flops=30_000_000_000,bytes_accessed=12<<20,transcendentals=4<<20))(lens,x,gm,g.reshape(1,D),b.reshape(1,D),w,wo,qt,k,v,ht,l)


def phi_pair(v):
    a=jnp.abs(v)
    t=1.0/(1.0+(0.3275911*0.7071067811865476)*a)
    e=jnp.exp2(v*v*(-0.5*LOG2E))
    y=t*(0.5*0.254829592+t*(0.5*-0.284496736+t*(0.5*1.421413741+t*(0.5*-1.453152027+t*(0.5*1.061405429)))))
    y=y*e
    return jnp.where(v<0,y,1.0-y), e*0.3989422804014327

def ln_back(dn,xh,r,gain):
    gd=dn*gain
    return r*(gd-jnp.mean(gd,axis=-1,keepdims=True)-xh*jnp.mean(gd*xh,axis=-1,keepdims=True))

def b_kernel(t, SB, cnt_ref, m_ref, cot_ref, g2_ref, b2_ref, w_ref, wo_ref, g3_ref, b3_ref, wu_ref, bu_ref, wd_ref, bd_ref,
             out_ref, gm_ref, dw_ref, dwo_ref, dwu_ref, dwd_ref, dv_ref, dbu_ref,
             n2_s, n3_s, r_s, ht_s, dpt_s, act_s, gp_s, cot_s, qt_s, k_s, v_s, e_s, dos_s):
    FA,_,D=m_ref.shape
    R=FA*SB
    H=D//64
    i=pl.program_id(0); last=pl.num_programs(0)-1
    rows=pl.ds(pl.multiple_of(i*R,R),R)
    m=m_ref[...].reshape(R,D).astype(F32)
    c,r2=ln_stats(m)
    xh2=c*r2
    n2=(xh2*g2_ref[...]+b2_ref[...]).astype(BF)
    n2_s[rows,:]=n2
    qt_s[...]=(dg(w_ref[:,0:D],n2,0,1)*QS).astype(BF)
    k_s[...]=dg(n2,w_ref[:,D:2*D],1,0).astype(BF)
    v_s[...]=dg(n2,w_ref[:,2*D:3*D],1,0).astype(BF)
    n=cnt_ref[t]
    krow=lax.broadcasted_iota(jnp.int32,(R,128),0)
    lane=lax.broadcasted_iota(jnp.int32,(R,128),1)
    kb=jnp.where(lane==0,jnp.where(krow//SB>=n,-1e30,0.0),jnp.where(lane-1==krow%SB,-1e30,0.0)).astype(BF)
    vb=jnp.where(lane<3,1.0,0.0).astype(BF)
    qcol=lax.broadcasted_iota(jnp.int32,(128,R),1)
    sub=lax.broadcasted_iota(jnp.int32,(128,R),0)
    qa=jnp.where((sub==0)|((sub<=SB)&(sub-1!=qcol%SB)),1.0,0.0).astype(BF)
    ones=jnp.ones((16,R),BF)
    rls=[]
    cols=pl.ds(pl.multiple_of(i*R,R),R)
    for p in range(D//128):
        kp=jnp.concatenate([k_s[:,p*128:p*128+128],kb],axis=1)
        vt=v_s[:,p*128:p*128+128].T
        for u in range(2):
            h=2*p+u
            s=dg(kp,pad_head(qt_s[h*64:h*64+64,:],u,qa),1,0)
            mx=jnp.max(s,axis=0,keepdims=True)
            e=jnp.exp2(s-mx).astype(BF)
            e_s[h]=e
            o=dg(jnp.concatenate([vt[u*64:u*64+64],ones],axis=0),e,1,0)
            rl=1.0/o[64:65]
            rls.append(rl)
            ht_s[h*64:h*64+64,cols]=(o[:64]*rl).astype(BF)
    m2=m+dg(ht_s[:,cols],wo_ref[...],0,0)
    c,r3=ln_stats(m2)
    xh3=c*r3
    n3=(xh3*g3_ref[...]+b3_ref[...]).astype(BF)
    n3_s[rows,:]=n3
    cot=cot_ref[...].reshape(R,D)
    cot_s[rows,:]=cot
    C=512
    dbu=[]
    for q in range(wu_ref.shape[1]//C):
        cs=slice(q*C,q*C+C)
        pre=dg(n3,wu_ref[:,cs],1,0)+bu_ref[:,cs]
        P,ph=phi_pair(pre)
        act_s[rows,cs]=(pre*P).astype(BF)
        gp=((P+pre*ph)*dg(cot,wd_ref[cs,:],1,1)).astype(BF)
        gp_s[rows,cs]=gp
        dbu.append(jnp.sum(gp.astype(F32),axis=0,keepdims=True))
    out=m2+dg(act_s[rows,:],wd_ref[...],1,0)+bd_ref[...]
    out_ref[...]=out.astype(BF).reshape(FA,SB,D)
    dn3=dg(gp_s[rows,:],wu_ref[...],1,1)
    dg3=jnp.sum(dn3*xh3,axis=0,keepdims=True)
    db3=jnp.sum(dn3,axis=0,keepdims=True)
    cotf=cot.astype(F32)
    gm2=cotf+ln_back(dn3,xh3,r3,g3_ref[...])
    rr=gm2.astype(BF)
    r_s[rows,:]=rr
    dot=dg(wo_ref[...],rr,1,1)
    for p in range(D//128):
        vp=jnp.concatenate([v_s[:,p*128:p*128+128],vb],axis=1)
        kt=k_s[:,p*128:p*128+128].T
        for u in range(2):
            h=2*p+u
            hs=slice(h*64,h*64+64)
            rl=rls[h]
            do=dot[hs,:]
            dd=jnp.sum(do*ht_s[hs,cols].astype(F32),axis=0,keepdims=True)*rl
            dob=(do*rl).astype(BF)
            d3=[-z.astype(F32) for z in split3(dd)]
            dp=dg(vp,pad_head(dob,u,row_block(d3,R)),1,0)
            e=e_s[h]
            ds=(e.astype(F32)*dp).astype(BF)
            dpt_s[2*D+h*64:2*D+h*64+64,cols]=dg(dob,e,1,1).astype(BF)
            dpt_s[D+h*64:D+h*64+64,cols]=(dg(qt_s[hs,:],ds,1,1)*LN2).astype(BF)
            dpt_s[h*64:h*64+64,cols]=(dg(kt[u*64:u*64+64],ds,1,0)*0.125).astype(BF)
    dn2=dg(dpt_s[:,cols],w_ref[...],0,1).astype(BF).astype(F32)
    dg2=jnp.sum(dn2*xh2,axis=0,keepdims=True)
    db2=jnp.sum(dn2,axis=0,keepdims=True)
    gm_ref[...]=(gm2+ln_back(dn2,xh2,r2,g2_ref[...])).astype(BF).reshape(FA,SB,D)
    small=[dg2,db2,dg3,db3,jnp.sum(cotf,axis=0,keepdims=True)]
    @pl.when(i==0)
    def _():
        dv_ref[...]=jnp.zeros_like(dv_ref)
        dbu_ref[...]=jnp.zeros_like(dbu_ref)
    for j,z in enumerate(small):
        dv_ref[j:j+1]+=z
    for q,z in enumerate(dbu):
        dbu_ref[0:1,q*C:q*C+C]+=z
    @pl.when(i==last)
    def _():
        dwo_ref[...]=dg(ht_s[...],r_s[...],1,0).astype(BF)
        for q in range(3):
            dw_ref[:,q*D:q*D+D]=dg(n2_s[...],dpt_s[q*D:q*D+D,:],0,1).astype(BF)
        for q in range(wu_ref.shape[1]//C):
            cs=slice(q*C,q*C+C)
            dwu_ref[:,cs]=dg(n3_s[...],gp_s[:,cs],0,0).astype(BF)
            dwd_ref[cs,:]=dg(act_s[:,cs],cot_s[...],0,0).astype(BF)

def run_b(t, cnt, m, cot, g2,b2,w,wo,g3,b3,wu,bu,wd,bd, SB=16):
    FA,SL,D=m.shape; FF=wu.shape[1]; R=FA*SB; N=FA*SL
    row=pl.BlockSpec((FA,SB,D),lambda i,s:(0,i,0))
    one=lambda *sh: pl.BlockSpec(sh,lambda i,s:(0,)*len(sh),pipeline_mode=pl.Buffered(1))
    con=lambda *sh: pl.BlockSpec(sh,lambda i,s:(0,)*len(sh))
    gs=pltpu.PrefetchScalarGridSpec(num_scalar_prefetch=1,grid=(SL//SB,),
        in_specs=[row,row,one(1,D),one(1,D),one(D,3*D),one(D,D),one(1,D),one(1,D),one(D,FF),one(1,FF),one(FF,D),one(1,D)],
        out_specs=[row,row,con(D,3*D),con(D,D),con(D,FF),con(FF,D),con(8,D),con(8,FF)],
        scratch_shapes=[pltpu.VMEM((N,D),BF),pltpu.VMEM((N,D),BF),pltpu.VMEM((N,D),BF),pltpu.VMEM((D,N),BF),pltpu.VMEM((3*D,N),BF),
            pltpu.VMEM((N,FF),BF),pltpu.VMEM((N,FF),BF),pltpu.VMEM((N,D),BF),
            pltpu.VMEM((D,R),BF),pltpu.VMEM((R,D),BF),pltpu.VMEM((R,D),BF),pltpu.VMEM((D//64,R,R),BF),pltpu.VMEM((8,128),F32)])
    sd=jax.ShapeDtypeStruct
    r=lambda z:z.reshape(1,-1)
    return pl.pallas_call(partial(b_kernel,t,SB),grid_spec=gs,
        out_shape=[sd((FA,SL,D),BF),sd((FA,SL,D),BF),sd((D,3*D),BF),sd((D,D),BF),sd((D,FF),BF),sd((FF,D),BF),sd((8,D),F32),sd((8,FF),F32)],
        compiler_params=pltpu.CompilerParams(vmem_limit_bytes=60<<20),name="middle",
        cost_estimate=pl.CostEstimate(flops=50_000_000_000,bytes_accessed=20<<20,transcendentals=4<<20))(cnt,m,cot,r(g2),r(b2),w,wo,r(g3),r(b3),wu,r(bu),wd,r(bd))

from jax.sharding import PartitionSpec as P


def gather_sum(pieces):
    total=pieces[0].astype(F32)
    for z in pieces[1:]:
        total=total+z.astype(F32)
    return total

def pick(a,i,axis=0):
    return lax.dynamic_index_in_dim(a,i,axis,keepdims=False)

def reduce_rows(g):
    nf,rw,D=g.shape
    nt=lax.axis_size("task")
    f=lax.axis_index("feat"); t=lax.axis_index("task")
    c=f%2; z=f//2; nz=nf//2
    gp=g.reshape(nz,2,rw,D)
    got=lax.ppermute(pick(gp,1-c,1),"feat",[(i,i^1) for i in range(nf)])
    s=gather_sum([pick(gp,c,1),got]).astype(BF).reshape(nz,nt,rw//nt,D)
    s=gather_sum([pick(s,t,1)]+[lax.ppermute(pick(s,t^r,1),"task",[(i,i^r) for i in range(nt)]) for r in range(1,nt)]).astype(BF)
    s=gather_sum([pick(s,z)]+[lax.ppermute(pick(s,z^r),"feat",[(i,i^(2*r)) for i in range(nf)]) for r in range(1,nz)]).astype(BF)
    every=jnp.stack([s]+[lax.ppermute(s,"task",[(i,i^r) for i in range(nt)]) for r in range(1,nt)])
    every=jnp.concatenate([pick(every,t^i)[None] for i in range(nt)])
    return every.reshape(rw,D).astype(F32)

def middle_plain(t,cnt,m,cot,g2,b2,w,wo,g3,b3,wu,bu,wd,bd):
    FA=m.shape[0]; D=m.shape[-1]; H=D//64
    mf=m.astype(F32)
    def norm(v,g,b):
        c,r=ln_stats(v)
        return c*r*g+b
    mm=lambda a,b: jnp.einsum("fsd,de->fse",a,b,preferred_element_type=F32)
    mt=lambda a,b: jnp.einsum("fse,de->fsd",a,b,preferred_element_type=F32)
    out_sum=lambda a,b: jnp.einsum("fsd,fse->de",a,b,preferred_element_type=F32).astype(BF)
    n2=norm(mf,g2,b2).astype(BF)
    q,k,v=[z[...,0,:,:] for z in jnp.split(mm(n2,w).astype(BF).reshape(m.shape[:2]+(3,H,64)),3,axis=2)]
    keep=jnp.arange(FA)<cnt[t]
    s=jnp.where(keep,jnp.einsum("qshe,kshe->shqk",q,k,preferred_element_type=F32)*0.125,-1e30)
    pr=jax.nn.softmax(s,axis=-1)
    h2=jnp.einsum("shqk,kshe->qshe",pr.astype(BF),v,preferred_element_type=F32).astype(BF).reshape(m.shape)
    m2=mf+mm(h2,wo)
    n3,back3=jax.vjp(norm,m2,g3,b3)
    n3=n3.astype(BF)
    pre=mm(n3,wu)+bu
    act,back=jax.vjp(partial(jax.nn.gelu,approximate=False),pre)
    act=act.astype(BF)
    out=(m2+mm(act,wd)+bd).astype(BF)
    gp=back(mt(cot,wd))[0].astype(BF)
    a,dg3,db3=back3(mt(gp,wu))
    gm2=cot.astype(F32)+a
    rr=gm2.astype(BF)
    do=mt(rr,wo).astype(BF).reshape(q.shape)
    dp=jnp.einsum("qshe,kshe->shqk",do,v,preferred_element_type=F32)
    ds=(pr*(dp-jnp.sum(pr*dp,axis=-1,keepdims=True))).astype(BF)
    dq=jnp.einsum("shqk,kshe->qshe",ds,k,preferred_element_type=F32)*0.125
    dk=jnp.einsum("shqk,qshe->kshe",ds,q,preferred_element_type=F32)*0.125
    dv=jnp.einsum("shqk,qshe->kshe",pr.astype(BF),do,preferred_element_type=F32)
    dpk=jnp.stack([dq,dk,dv],axis=2).reshape(m.shape[:2]+(3*D,)).astype(BF)
    _,back2=jax.vjp(norm,mf,g2,b2)
    a,dg2,db2=back2(mt(dpk,w).astype(BF).astype(F32))
    small=jnp.concatenate([jnp.stack([dg2,db2,dg3,db3,jnp.sum(cot.astype(F32),axis=(0,1))]),jnp.zeros((3,D),F32)])
    dbu=jnp.sum(gp.astype(F32),axis=(0,1))[None]
    return out,(gm2+a).astype(BF),out_sum(n2,dpk),out_sum(h2,rr),out_sum(n3,gp),out_sum(act,cot),small,dbu

def move(a):
    return lax.all_to_all(a,"feat",0,0)

def body(x,cot,lens,cnt,g1,b1,w1,wo1,g2,b2,w2,wo2,g3,b3,wu,bu,wd,bd):
    T,F,S,D=x.shape
    FF=wu.shape[1]
    nf=lax.axis_size("feat")
    sl=S//nf; FA=F*nf
    chunk=lambda a: a.reshape(nf,F,sl,D)
    spread=lambda a: a.reshape(F,nf,sl,D).swapaxes(0,1)
    rejoin=lambda a: a.swapaxes(0,1).reshape(F,S,D)
    cots=[move(spread(cot[t])) for t in range(T)]
    saved=[]; mids=[]
    for t in range(T):
        o=run_a(t,lens,x,g1,b1,w1,wo1,nf)
        mids.append(move(o[0])); saved.append(o[1:])
    mid_fn=run_b if FA*16<=256 else middle_plain
    outs=[]; gms=[]; mg=[]
    for t in range(T):
        o=mid_fn(t,cnt,mids[t].reshape(FA,sl,D),cots[t].reshape(FA,sl,D),g2,b2,w2,wo2,g3,b3,wu,bu,wd,bd)
        gms.append(move(chunk(o[1])))
        outs.append(move(chunk(o[0])))
        mg.append(o[2:])
    add=lambda i: gather_sum([m[i] for m in mg])
    rp=D//nf; fp=FF//nf
    blocks=lambda a: a.reshape(nf,rp,a.shape[1]//D,D).swapaxes(1,2).reshape(nf,-1,D)
    def with_vectors(mats,vecs):
        v=jnp.concatenate([z.reshape(-1,D) for z in vecs])
        v=jnp.pad(v,((0,32-v.shape[0]),(0,0)))
        return jnp.concatenate([z.astype(BF) for z in mats]+[jnp.broadcast_to(v.astype(BF)[None],(nf,)+v.shape)],axis=1)
    gmid=with_vectors([blocks(add(0)),blocks(add(1)),blocks(add(2)),add(3).reshape(nf,fp,D)],[add(4)[:5],add(5)[:1]])
    rmid=reduce_rows(gmid)
    dxs=[]; cg=[]
    for t in range(T):
        o=run_c(t,lens,x,gms[t],g1,b1,w1,wo1,*saved[t])
        dxs.append(o[0]); cg.append(o[1:])
    addc=lambda i: gather_sum([m[i] for m in cg])
    rlate=reduce_rows(with_vectors([blocks(addc(0)),blocks(addc(1))],[addc(2)[:2]]))
    f=lax.axis_index("feat")
    unblock=lambda a: a.reshape(-1,rp,D).swapaxes(0,1).reshape(rp,-1)
    vec=lambda a,i: lax.dynamic_slice_in_dim(a[i],f*rp,rp)
    ml=4*rp
    mm=8*rp+fp
    mv=rmid[mm:]; lv=rlate[ml:]
    dbu=lax.dynamic_slice_in_dim(mv[5:5+FF//D].reshape(FF),f*fp,fp)
    return (jnp.stack([rejoin(o) for o in outs]), jnp.stack(dxs),
        vec(lv,0),vec(lv,1),unblock(rlate[:3*rp]),unblock(rlate[3*rp:4*rp]),
        vec(mv,0),vec(mv,1),unblock(rmid[:3*rp]),unblock(rmid[3*rp:4*rp]),
        vec(mv,2),vec(mv,3),unblock(rmid[4*rp:8*rp]),dbu,rmid[8*rp:8*rp+fp],vec(mv,4))

def solution(mesh):
    rows=P("task","feat",None,None)
    mat=P("feat",None)
    return jax.shard_map(body,mesh=mesh,
        in_specs=(rows,rows,P("task"),P("task"))+(P(),)*14,
        out_specs=(rows,rows,P("feat"),P("feat"),mat,mat,P("feat"),P("feat"),mat,mat,P("feat"),P("feat"),mat,P("feat"),mat,P("feat")),
        check_vma=False)
```

time: 1100 us -> 429 us (0.39)
  matrix products: 286 us -> 0 us
  waiting for transfers between devices: 393 us -> 111 us
  Pallas kernels: 0 us -> 182 us
  other arithmetic: 165 us -> 24.2 us
  local copies, waits for them, and re-layouts: 168 us -> 43.3 us
  starting transfers between devices: 20.8 us -> 58.9 us
  blocking collectives: 36.5 us -> 0 us
  between operations: 16.6 us -> 1.4 us
    all_to_all x4 -> x8, waiting for transfers between devices: 393 us -> 54.1 us  [move(): return lax.all_to_all(a, 'feat', 0, 0)]
    dot_general x30 -> x0, matrix products: 286 us -> none  [the longest x6 49.6 us: back_project(): jnp.einsum('tfse,de->tfsd', left, matrix, preferred_element_type=jnp.floa...]
    pallas_call x0 -> x6, Pallas kernels: none -> 182 us  [the longest x2 109 us: run_b(): pl.pallas_call(partial(b_kernel, t, SB), grid_spec=gs, out_shape=[sd((FA,...]
    convert_element_type x26 -> x14, other arithmetic: 115 us -> 18.2 us  [the longest x6 10 us: with_vectors(): z.astype(BF)]
    ppermute x0 -> x20, waiting for transfers between devices: none -> 56.7 us  [the longest x6 27.3 us: reduce_rows(): lax.ppermute(s, 'task', [(i, i ^ r) for i in range(nt)])]
    convert_element_type x5 -> x6, local copies, waits for them, and re-layouts: 64.8 us -> 16.4 us  [with_vectors(): z.astype(BF)]
    reduce_sum x11 -> x0, other arithmetic: 38.9 us -> none  [the longest x2 17.8 us: attend(): totals = jnp.sum(exp_terms, axis=-1, keepdims=True)]
    reshape x4, local copies, waits for them, and re-layouts: 34.4 us -> 1.39 us  [the longest x3 1.38 us: body(): unblock = lambda a: a.reshape(-1, rp, D).swapaxes(0, 1).reshape(rp, -1)]
  transfers between devices with their start and end apart: 11 -> 28, of which waited for: 4 -> 15; matrix products, arithmetic and copies ran while one was open for 28% -> 12% of each run, Pallas kernels for 0% -> 43%
where the time goes in v1:
time: 429 us; the launch traced here: 421 us
  Pallas kernels  182 us (42%)
  waiting for transfers between devices  111 us (26%)
  starting transfers between devices  58.9 us (14%)
  local copies, waits for them, and re-layouts  43.3 us (10%)
  other arithmetic  24.2 us (6%)
    pallas_call x2, Pallas kernels, run_b(): pl.pallas_call(partial(b_kernel, t, SB), grid_spec=gs, out_shape=[sd((FA,...  109 us
    all_to_all x8, waiting for transfers between devices, move(): return lax.all_to_all(a, 'feat', 0, 0)  54.1 us
    pallas_call x2, Pallas kernels, run_c(): pl.pallas_call(partial(c_kernel, t), grid_spec=gs, out_shape=[sd((F, S, D...  44.4 us
    all_to_all x8, starting transfers between devices, move(): return lax.all_to_all(a, 'feat', 0, 0)  35.7 us
    pallas_call x2, Pallas kernels, run_a(): pl.pallas_call(partial(a_kernel, t), grid_spec=grid_spec, out_shape=[sd((...  28.8 us
    ppermute x6, waiting for transfers between devices, reduce_rows(): lax.ppermute(s, 'task', [(i, i ^ r) for i in range(nt)])  27.3 us
    ppermute x6, waiting for transfers between devices, reduce_rows(): lax.ppermute(pick(s, z ^ r), 'feat', [(i, i ^ 2 * r) for i in range(nf)])  18.6 us
    convert_element_type x6, local copies, waits for them, and re-layouts, with_vectors(): z.astype(BF)  16.4 us
  transfers between devices with their start and end apart: 28, of which 15 were waited for; matrix products, arithmetic and copies ran while one was open for 12% of the time, Pallas kernels for 43%

profile of v1, /device:TPU:0, one launch (start us, length us, event | category | flops | bytes accessed | tf_op | source)
XLA Modules:
  0.0 420.7 jit_solution(15497438772994741317)
XLA Ops:
  0.6 1.7 fusion.28
  3.5 6.3 %all-to-all-start.4 = ((bf16[8,2,64,512]{3,2,1,0:T(8,128)(2,1)}), bf16[8,2,64,512]{3,2,1,0:T(8,128)(2,1)S(1)}, u32[]{:S(2)}, u32[]{:S(2)}) async-start(bf16[8,2,64,512]{3,2,1,0:T(8,128)(2,1)} %bitcast.131), calls=%async_computation.4 | async-start | bytes 2097152 | tf_op jit(solution)/shard_map/all_to_all | solution.py:379
  10.9 25.5 %all-to-all-done.4 = bf16[8,2,64,512]{3,2,1,0:T(8,128)(2,1)S(1)} async-done(((bf16[8,2,64,512]{3,2,1,0:T(8,128)(2,1)}), bf16[8,2,64,512]{3,2,1,0:T(8,128)(2,1)S(1)}, u32[]{:S(2)}, u32[]{:S(2)}) %all-to-all-start.4) | async-done | bytes 1048608 | tf_op jit(solution)/shard_map/all_to_all | solution.py:379
  36.4 3.6 all-to-all-start.1
  39.9 14.4 %fwd_samples.2 = (bf16[8,2,64,512]{3,2,1,0:T(8,128)(2,1)}, bf16[2,512,512]{2,1,0:T(8,128)(2,1)}, bf16[2,512,512]{2,1,0:T(8,128)(2,1)}, bf16[2,512,512]{2,1,0:T(8...) custom-call(s32[2]{0:T(128)} %len_ref.7, bf16[2,2,512,512]{3,2,1,0:T(8,128)(2,1)} %x_ref.7, ...), custom_call_target="tpu_custom_call" | custom-call | flops 20000000000 | bytes 8388608 | tf_op jit(solution)/shard_map/fwd_samples/pallas_call | solution.py:90
  54.4 12.1 %all-to-all-done.1 = bf16[8,2,64,512]{3,2,1,0:T(8,128)(2,1)S(1)} async-done(((bf16[8,2,64,512]{3,2,1,0:T(8,128)(2,1)}), bf16[8,2,64,512]{3,2,1,0:T(8,128)(2,1)S(1)}, u32[]{:S(2)}, u32[]{:S(2)}) %all-to-all-start.1) | async-done | bytes 1048608 | tf_op jit(solution)/shard_map/all_to_all | solution.py:379
  66.5 3.6 all-to-all-start
  70.0 14.4 %fwd_samples.3 = (bf16[8,2,64,512]{3,2,1,0:T(8,128)(2,1)}, bf16[2,512,512]{2,1,0:T(8,128)(2,1)}, bf16[2,512,512]{2,1,0:T(8,128)(2,1)}, bf16[2,512,512]{2,1,0:T(8...) custom-call(s32[2]{0:T(128)} %len_ref.7, bf16[2,2,512,512]{3,2,1,0:T(8,128)(2,1)} %x_ref.7, ...), custom_call_target="tpu_custom_call" | custom-call | flops 20000000000 | bytes 8388608 | tf_op jit(solution)/shard_map/fwd_samples/pallas_call | solution.py:90
  84.5 12.1 %all-to-all-done = bf16[8,2,64,512]{3,2,1,0:T(8,128)(2,1)S(1)} async-done(((bf16[8,2,64,512]{3,2,1,0:T(8,128)(2,1)}), bf16[8,2,64,512]{3,2,1,0:T(8,128)(2,1)S(1)}, u32[]{:S(2)}, u32[]{:S(2)}) %all-to-all-start) | async-done | bytes 1048608 | tf_op jit(solution)/shard_map/all_to_all | solution.py:379
  96.5 3.6 all-to-all-start.3
  100.1 54.5 %middle.2 = (bf16[16,64,512]{2,1,0:T(8,128)(2,1)}, bf16[16,64,512]{2,1,0:T(8,128)(2,1)}, bf16[512,1536]{1,0:T(8,128)(2,1)}, bf16[512,512]{1,0:T(8,128)(2,1)}, bf...) custom-call(s32[2]{0:T(128)} %cnt_ref.3, ...), custom_call_target="tpu_custom_call" | custom-call | flops 49999998976 | bytes 20971520 | tf_op jit(solution)/shard_map/middle/pallas_call | solution.py:308
  154.7 5.0 %all-to-all-start.6 = ((bf16[8,2,64,512]{3,2,1,0:T(8,128)(2,1)}), bf16[8,2,64,512]{3,2,1,0:T(8,128)(2,1)S(1)}, u32[]{:S(2)}, u32[]{:S(2)}) async-start(bf16[8,2,64,512]{3,2,1,0:T(8,128)(2,1)} %bitcast.158), calls=%async_computation.6 | async-start | bytes 2097152 | tf_op jit(solution)/shard_map/all_to_all | solution.py:379
  159.7 54.4 %middle.3 = (bf16[16,64,512]{2,1,0:T(8,128)(2,1)}, bf16[16,64,512]{2,1,0:T(8,128)(2,1)}, bf16[512,1536]{1,0:T(8,128)(2,1)}, bf16[512,512]{1,0:T(8,128)(2,1)}, bf...) custom-call(s32[2]{0:T(128)} %cnt_ref.3, ...), custom_call_target="tpu_custom_call" | custom-call | flops 49999998976 | bytes 20971520 | tf_op jit(solution)/shard_map/middle/pallas_call | solution.py:308
  215.0 3.0 add_convert_fusion.1
  218.0 2.8 convert_element_type.235
  220.8 3.6 copy.61
  224.4 1.5 add_convert_fusion.2
  225.9 4.6 %convert_element_type.225 = bf16[8,64,3,512]{3,2,1,0:T(4,128)(2,1)S(1)} reshape(bf16[512,1536]{1,0:T(8,128)(2,1)} %add_convert_fusion.2) | data formatting | bytes 3145728 | tf_op jit(solution)/shard_map/convert_element_type | solution.py:407
  236.0 2.1 dynamic-slice_bitcast_fusion
  238.1 1.5 copy-done
  240.2 4.7 %all-to-all-start.7 = ((bf16[8,2,64,512]{3,2,1,0:T(8,128)(2,1)}), bf16[8,2,64,512]{3,2,1,0:T(8,128)(2,1)S(1)}, u32[]{:S(2)}, u32[]{:S(2)}) async-start(bf16[8,2,64,512]{3,2,1,0:T(8,128)(2,1)} %bitcast.24), calls=%async_computation.7 | async-start | bytes 2097152 | tf_op jit(solution)/shard_map/all_to_all | solution.py:379
  244.9 22.2 %bwd_samples.2 = (bf16[2,512,512]{2,1,0:T(8,128)(2,1)}, f32[512,1536]{1,0:T(8,128)}, f32[512,512]{1,0:T(8,128)}, f32[8,512]{1,0:T(8,128)}) custom-call(s32[2]{0:T(128)} %len_ref.7, bf16[2,2,512,512]{3,2,1,0:T(8,128)(2,1)} %x_ref.7, bf16[8,2,64,512]{3,2,1,0:T(8,128)(2,1)} %copy-done.9, f32[1,512]{1,0:T(1,128)} %bitcast.190, f32[1,512]{1,0:T(1,128)} %bitcast.194, ...), custom_call_target="tpu_custom_call" | custom-call | flops 30000001024 | bytes 12582912 | tf_op jit(solution)/shard_map/bwd_samples/pallas_call | solution.py:170
  267.1 4.4 %all-to-all-done.7.gm_ref = bf16[8,2,64,512]{3,2,1,0:T(8,128)(2,1)S(1)} async-done(((bf16[8,2,64,512]{3,2,1,0:T(8,128)(2,1)}), bf16[8,2,64,512]{3,2,1,0:T(8,128)(2,1)S(1)}, u32[]{:S(2)}, u32[]{:S(2)}) %all-to-all-start.7) | async-done | bytes 1048608 | tf_op jit(solution)/shard_map/all_to_all | solution.py:379
  271.5 4.0 all-to-all-start.2
  275.5 22.2 %bwd_samples.3 = (bf16[2,512,512]{2,1,0:T(8,128)(2,1)}, f32[512,1536]{1,0:T(8,128)}, f32[512,512]{1,0:T(8,128)}, f32[8,512]{1,0:T(8,128)}) custom-call(s32[2]{0:T(128)} %len_ref.7, bf16[2,2,512,512]{3,2,1,0:T(8,128)(2,1)} %x_ref.7, bf16[8,2,64,512]{3,2,1,0:T(8,128)(2,1)} %copy-done.12, f32[1,512]{1,0:T(1,128)} %bitcast.191, f32[1,512]{1,0:T(1,128)} %bitcast.195, ...), custom_call_target="tpu_custom_call" | custom-call | flops 30000001024 | bytes 12582912 | tf_op jit(solution)/shard_map/bwd_samples/pallas_call | solution.py:170
  297.7 4.4 %add_convert_fusion.3 = bf16[512,1536]{1,0:T(8,128)(2,1)} fusion(f32[512,1536]{1,0:T(8,128)} %get-tuple-element.70, f32[512,1536]{1,0:T(8,128)} %get-tuple-element.71), kind=kLoop, calls=%fused_computation.6 | loop fusion | flops 1572864 | bytes 7864320 | tf_op jit(solution)/shard_map/convert_element_type | solution.py:407
  302.1 4.6 %convert_element_type.199 = bf16[8,64,3,512]{3,2,1,0:T(4,128)(2,1)S(1)} reshape(bf16[512,1536]{1,0:T(8,128)(2,1)} %add_convert_fusion.3) | data formatting | bytes 3145728 | tf_op jit(solution)/shard_map/convert_element_type | solution.py:407
  310.2 5.0 %all-to-all-start.5 = ((bf16[8,2,64,512]{3,2,1,0:T(8,128)(2,1)}), bf16[8,2,64,512]{3,2,1,0:T(8,128)(2,1)}, u32[]{:S(2)}, u32[]{:S(2)}) async-start(bf16[8,2,64,512]{3,2,1,0:T(8,128)(2,1)} %bitcast.156), calls=%async_computation.5 | async-start | bytes 2097152 | tf_op jit(solution)/shard_map/all_to_all | solution.py:379
  315.3 1.6 fusion.1
  317.0 1.6 collective-permute-start.1
  320.6 3.9 fusion
  324.5 2.4 collective-permute-done.1
  326.9 7.0 %collective-permute-done.3 = bf16[4,72,512]{2,1,0:T(8,128)(2,1)S(1)} collective-permute-done((bf16[4,72,512]{2,1,0:T(8,128)(2,1)S(1)}, bf16[4,72,512]{2,1,0:T(8,128)(2,1)S(1)}, u32[]{:S(2)}, u32[]{:S(2)}) %collective-permute-start.3) | collective-permute-done | bytes 294944 | tf_op jit(solution)/shard_map/ppermute | solution.py:333
  335.5 1.7 collective-permute-start.4
  337.2 2.4 collective-permute-start.6
  339.6 1.5 dynamic-slice_bitcast_fusion.4
  344.6 3.6 collective-permute-done.5
  348.2 2.5 collective-permute-start.9
  350.7 2.3 copy.55
  355.1 23.4 %collective-permute-done.9 = bf16[72,512]{1,0:T(8,128)(2,1)S(1)} collective-permute-done((bf16[72,512]{1,0:T(8,128)(2,1)S(1)}, bf16[72,512]{1,0:T(8,128)(2,1)S(1)}, u32[]{:S(2)}, u32[]{:S(2)}) %collective-permute-start.9) | collective-permute-done | bytes 73760 | tf_op jit(solution)/shard_map/ppermute | solution.py:335
  379.9 3.6 pad_maximum_fusion.1
  383.7 2.1 fusion.4
  387.3 2.4 collective-permute-start.16
  389.8 3.7 collective-permute-done.14
  393.5 3.9 collective-permute-done.16
  397.4 6.6 %collective-permute-done.15 = bf16[200,512]{1,0:T(8,128)(2,1)S(1)} collective-permute-done((bf16[200,512]{1,0:T(8,128)(2,1)S(1)}, bf16[200,512]{1,0:T(8,128)(2,1)S(1)}, u32[]{:S(2)}, u32[]{:S(2)}) %collective-permute-start.15) | collective-permute-done | bytes 204832 | tf_op jit(solution)/shard_map/ppermute | solution.py:334
  410.0 1.9 collective-permute-done.19
  411.9 2.0 collective-permute-done.18
  (126 shorter events, 37.5 us)
Async XLA Ops:
  3.5 32.9 %all-to-all-start.4 = ((bf16[8,2,64,512]{3,2,1,0:T(8,128)(2,1)}), bf16[8,2,64,512]{3,2,1,0:T(8,128)(2,1)S(1)}, u32[]{:S(2)}, u32[]{:S(2)}) async-start(bf16[8,2,64,512]{3,2,1,0:T(8,128)(2,1)} %bitcast.131), calls=%async_computation.4 | async-start | bytes 2097152 | tf_op jit(solution)/shard_map/all_to_all | solution.py:379
  36.4 18.0 %copy-start.8 = (bf16[8,2,64,512]{3,2,1,0:T(8,128)(2,1)}, bf16[8,2,64,512]{3,2,1,0:T(8,128)(2,1)S(1)}, u32[]{:S(2)}) copy-start(bf16[8,2,64,512]{3,2,1,0:T(8,128)(2,1)S(1)} %all-to-all-done.4) | copy-start | bytes 3145732
  36.4 30.1 %all-to-all-start.1 = ((bf16[8,2,64,512]{3,2,1,0:T(8,128)(2,1)}), bf16[8,2,64,512]{3,2,1,0:T(8,128)(2,1)S(1)}, u32[]{:S(2)}, u32[]{:S(2)}) async-start(bf16[8,2,64,512]{3,2,1,0:T(8,128)(2,1)} %bitcast.132), calls=%async_computation.1 | async-start | bytes 2097152 | tf_op jit(solution)/shard_map/all_to_all | solution.py:379
  66.5 18.0 %copy-start.10 = (bf16[8,2,64,512]{3,2,1,0:T(8,128)(2,1)}, bf16[8,2,64,512]{3,2,1,0:T(8,128)(2,1)S(1)}, u32[]{:S(2)}) copy-start(bf16[8,2,64,512]{3,2,1,0:T(8,128)(2,1)S(1)} %all-to-all-done.1) | copy-start | bytes 3145732
  66.5 30.1 %all-to-all-start = ((bf16[8,2,64,512]{3,2,1,0:T(8,128)(2,1)}), bf16[8,2,64,512]{3,2,1,0:T(8,128)(2,1)S(1)}, u32[]{:S(2)}, u32[]{:S(2)}) async-start(bf16[8,2,64,512]{3,2,1,0:T(8,128)(2,1)} %get-tuple-element.52), calls=%async_computation | async-start | bytes 2097152 | tf_op jit(solution)/shard_map/all_to_all | solution.py:379
  96.5 3.6 copy-start.14
  96.5 58.1 %all-to-all-start.3 = ((bf16[8,2,64,512]{3,2,1,0:T(8,128)(2,1)}), bf16[8,2,64,512]{3,2,1,0:T(8,128)(2,1)S(1)}, u32[]{:S(2)}, u32[]{:S(2)}) async-start(bf16[8,2,64,512]{3,2,1,0:T(8,128)(2,1)} %get-tuple-element.54), calls=%async_computation.3 | async-start | bytes 2097152 | tf_op jit(solution)/shard_map/all_to_all | solution.py:379
  154.7 5.0 %copy-start.13 = (bf16[8,2,64,512]{3,2,1,0:T(8,128)(2,1)}, bf16[8,2,64,512]{3,2,1,0:T(8,128)(2,1)S(1)}, u32[]{:S(2)}) copy-start(bf16[8,2,64,512]{3,2,1,0:T(8,128)(2,1)S(1)} %all-to-all-done.3) | copy-start | bytes 3145732
  154.7 85.5 %all-to-all-start.6 = ((bf16[8,2,64,512]{3,2,1,0:T(8,128)(2,1)}), bf16[8,2,64,512]{3,2,1,0:T(8,128)(2,1)S(1)}, u32[]{:S(2)}, u32[]{:S(2)}) async-start(bf16[8,2,64,512]{3,2,1,0:T(8,128)(2,1)} %bitcast.158), calls=%async_computation.6 | async-start | bytes 2097152 | tf_op jit(solution)/shard_map/all_to_all | solution.py:379
  220.8 3.6 copy-start.6
  220.8 3.6 copy-start.7
  230.9 0.7 copy-start.20
  230.9 1.1 copy-start.17
  231.0 1.2 copy-start.18
  231.1 1.8 copy-start.1
  232.9 1.6 copy-start.4
  232.9 2.2 copy-start.5
  236.0 3.7 copy-start
  239.7 80.9 %collective-permute-start.10 = (bf16[4,800,512]{2,1,0:T(8,128)(2,1)}, bf16[4,800,512]{2,1,0:T(8,128)(2,1)}, u32[]{:S(2)}, u32[]{:S(2)}) collective-permute-start(bf16[4,800,512]{2,1,0:T(8,128)(2,1)} %dynamic-slice_bitcast_fusion), channel_id=1, source_target_pairs={{0,1},{1,0},{2,3},{3,2},{4,5},{5,4},{6,7},{7,6},{8,9},{9,8},{10,11... | collective-permute-start | bytes 9830408 | tf_op jit(solution)/shard_map/ppermute | solution.py:331
  240.2 4.7 %copy-start.9 = (bf16[8,2,64,512]{3,2,1,0:T(8,128)(2,1)}, bf16[8,2,64,512]{3,2,1,0:T(8,128)(2,1)S(1)}, u32[]{:S(2)}) copy-start(bf16[8,2,64,512]{3,2,1,0:T(8,128)(2,1)S(1)} %all-to-all-done.6.gm_ref) | copy-start | bytes 3145732
  240.2 31.3 %all-to-all-start.7 = ((bf16[8,2,64,512]{3,2,1,0:T(8,128)(2,1)}), bf16[8,2,64,512]{3,2,1,0:T(8,128)(2,1)S(1)}, u32[]{:S(2)}, u32[]{:S(2)}) async-start(bf16[8,2,64,512]{3,2,1,0:T(8,128)(2,1)} %bitcast.24), calls=%async_computation.7 | async-start | bytes 2097152 | tf_op jit(solution)/shard_map/all_to_all | solution.py:379
  271.5 4.0 copy-start.12
  271.5 38.7 %all-to-all-start.2 = ((bf16[8,2,64,512]{3,2,1,0:T(8,128)(2,1)}), bf16[8,2,64,512]{3,2,1,0:T(8,128)(2,1)S(1)}, u32[]{:S(2)}, u32[]{:S(2)}) async-start(bf16[8,2,64,512]{3,2,1,0:T(8,128)(2,1)} %bitcast.12), calls=%async_computation.2 | async-start | bytes 2097152 | tf_op jit(solution)/shard_map/all_to_all | solution.py:379
  306.7 1.4 copy-start.11
  306.7 1.5 copy-start.15
  309.8 5.5 %collective-permute-start = (bf16[4,288,512]{2,1,0:T(8,128)(2,1)}, bf16[4,288,512]{2,1,0:T(8,128)(2,1)}, u32[]{:S(2)}, u32[]{:S(2)}) collective-permute-start(bf16[4,288,512]{2,1,0:T(8,128)(2,1)} %dynamic-slice_bitcast_fusion.1), channel_id=1, source_target_pairs={{0,1},{1,0},{2,3},{3,2},{4,5},{5,4},{6,7},{7,6},{8,9},{9,8},{10,11... | collective-permute-start | bytes 3538952 | tf_op jit(solution)/shard_map/ppermute | solution.py:331
  310.2 6.7 %copy-start.2 = (bf16[8,2,64,512]{3,2,1,0:T(8,128)(2,1)}, bf16[8,2,64,512]{3,2,1,0:T(8,128)(2,1)S(1)}, u32[]{:S(2)}) copy-start(bf16[8,2,64,512]{3,2,1,0:T(8,128)(2,1)S(1)} %all-to-all-done.2) | copy-start | bytes 3145732
  310.2 42.7 %all-to-all-start.5 = ((bf16[8,2,64,512]{3,2,1,0:T(8,128)(2,1)}), bf16[8,2,64,512]{3,2,1,0:T(8,128)(2,1)}, u32[]{:S(2)}, u32[]{:S(2)}) async-start(bf16[8,2,64,512]{3,2,1,0:T(8,128)(2,1)} %bitcast.156), calls=%async_computation.5 | async-start | bytes 2097152 | tf_op jit(solution)/shard_map/all_to_all | solution.py:379
  317.0 9.9 %collective-permute-start.1 = (bf16[4,72,512]{2,1,0:T(8,128)(2,1)S(1)}, bf16[4,72,512]{2,1,0:T(8,128)(2,1)S(1)}, u32[]{:S(2)}, u32[]{:S(2)}) collective-permute-start(bf16[4,72,512]{2,1,0:T(8,128)(2,1)S(1)} %get-tuple-element.100), channel_id=1, source_target_pairs={{0,8},{8,0},{16,24},{24,16},{1,9},{9,1},{17,25},{25,17},{2,10},{10... | collective-permute-start | bytes 884744 | tf_op jit(solution)/shard_map/ppermute | solution.py:333
  318.6 15.3 %collective-permute-start.3 = (bf16[4,72,512]{2,1,0:T(8,128)(2,1)S(1)}, bf16[4,72,512]{2,1,0:T(8,128)(2,1)S(1)}, u32[]{:S(2)}, u32[]{:S(2)}) collective-permute-start(bf16[4,72,512]{2,1,0:T(8,128)(2,1)S(1)} %get-tuple-element.101), channel_id=1, source_target_pairs={{0,24},{8,16},{16,8},{24,0},{1,25},{9,17},{17,9},{25,1},{2,26},{10... | collective-permute-start | bytes 884744 | tf_op jit(solution)/shard_map/ppermute | solution.py:333
  320.1 15.2 %collective-permute-start.2 = (bf16[4,72,512]{2,1,0:T(8,128)(2,1)S(1)}, bf16[4,72,512]{2,1,0:T(8,128)(2,1)S(1)}, u32[]{:S(2)}, u32[]{:S(2)}) collective-permute-start(bf16[4,72,512]{2,1,0:T(8,128)(2,1)S(1)} %get-tuple-element.102), channel_id=1, source_target_pairs={{0,16},{8,24},{16,0},{24,8},{1,17},{9,25},{17,1},{25,9},{2,18},{10... | collective-permute-start | bytes 884744 | tf_op jit(solution)/shard_map/ppermute | solution.py:333
  335.5 8.5 %collective-permute-start.4 = (bf16[72,512]{1,0:T(8,128)(2,1)S(1)}, bf16[72,512]{1,0:T(8,128)(2,1)S(1)}, u32[]{:S(2)}, u32[]{:S(2)}) collective-permute-start(bf16[72,512]{1,0:T(8,128)(2,1)S(1)} %get-tuple-element.116), channel_id=1, source_target_pairs={{0,2},{1,3},{2,0},{3,1},{4,6},{5,7},{6,4},{7,5},{8,10},{9,11},{10,... | collective-permute-start | bytes 221192 | tf_op jit(solution)/shard_map/ppermute | solution.py:334
  337.2 7.4 %collective-permute-start.6 = (bf16[72,512]{1,0:T(8,128)(2,1)S(1)}, bf16[72,512]{1,0:T(8,128)(2,1)S(1)}, u32[]{:S(2)}, u32[]{:S(2)}) collective-permute-start(bf16[72,512]{1,0:T(8,128)(2,1)S(1)} %get-tuple-element.117), channel_id=1, source_target_pairs={{0,6},{1,7},{2,4},{3,5},{4,2},{5,3},{6,0},{7,1},{8,14},{9,15},{10,... | collective-permute-start | bytes 221192 | tf_op jit(solution)/shard_map/ppermute | solution.py:334
  339.6 8.6 %collective-permute-start.5 = (bf16[72,512]{1,0:T(8,128)(2,1)S(1)}, bf16[72,512]{1,0:T(8,128)(2,1)S(1)}, u32[]{:S(2)}, u32[]{:S(2)}) collective-permute-start(bf16[72,512]{1,0:T(8,128)(2,1)S(1)} %get-tuple-element.118), channel_id=1, source_target_pairs={{0,4},{1,5},{2,6},{3,7},{4,0},{5,1},{6,2},{7,3},{8,12},{9,13},{10,... | collective-permute-start | bytes 221192 | tf_op jit(solution)/shard_map/ppermute | solution.py:334
  341.1 42.6 %collective-permute-start.11 = (bf16[4,200,512]{2,1,0:T(8,128)(2,1)}, bf16[4,200,512]{2,1,0:T(8,128)(2,1)}, u32[]{:S(2)}, u32[]{:S(2)}) collective-permute-start(bf16[4,200,512]{2,1,0:T(8,128)(2,1)} %get-tuple-element.88), channel_id=1, source_target_pairs={{0,8},{8,0},{16,24},{24,16},{1,9},{9,1},{17,25},{25,17},{2,10},{10... | collective-permute-start | bytes 2457608 | tf_op jit(solution)/shard_map/ppermute | solution.py:333
  342.6 41.1 %collective-permute-start.13 = (bf16[4,200,512]{2,1,0:T(8,128)(2,1)}, bf16[4,200,512]{2,1,0:T(8,128)(2,1)}, u32[]{:S(2)}, u32[]{:S(2)}) collective-permute-start(bf16[4,200,512]{2,1,0:T(8,128)(2,1)} %get-tuple-element.89), channel_id=1, source_target_pairs={{0,24},{8,16},{16,8},{24,0},{1,25},{9,17},{17,9},{25,1},{2,26},{10... | collective-permute-start | bytes 2457608 | tf_op jit(solution)/shard_map/ppermute | solution.py:333
  343.9 39.8 %collective-permute-start.12 = (bf16[4,200,512]{2,1,0:T(8,128)(2,1)}, bf16[4,200,512]{2,1,0:T(8,128)(2,1)}, u32[]{:S(2)}, u32[]{:S(2)}) collective-permute-start(bf16[4,200,512]{2,1,0:T(8,128)(2,1)} %get-tuple-element.90), channel_id=1, source_target_pairs={{0,16},{8,24},{16,0},{24,8},{1,17},{9,25},{17,1},{25,9},{2,18},{10... | collective-permute-start | bytes 2457608 | tf_op jit(solution)/shard_map/ppermute | solution.py:333
  348.2 30.2 %collective-permute-start.9 = (bf16[72,512]{1,0:T(8,128)(2,1)S(1)}, bf16[72,512]{1,0:T(8,128)(2,1)S(1)}, u32[]{:S(2)}, u32[]{:S(2)}) collective-permute-start(bf16[72,512]{1,0:T(8,128)(2,1)S(1)} %fusion.13), channel_id=1, source_target_pairs={{0,24},{8,16},{16,8},{24,0},{1,25},{9,17},{17,9},{25,1},{2,26},{10... | collective-permute-start | bytes 221192 | tf_op jit(solution)/shard_map/ppermute | solution.py:335
  353.0 26.9 %copy-start.3 = (bf16[2,8,64,512]{3,2,1,0:T(8,128)(2,1)S(1)}, bf16[2,8,64,512]{3,2,1,0:T(8,128)(2,1)}, u32[]{:S(2)}) copy-start(bf16[2,8,64,512]{3,2,1,0:T(8,128)(2,1)} %copy.55) | copy-start | bytes 3145732
  353.0 26.9 %copy-start.16 = (bf16[2,512,512]{2,1,0:T(8,128)(2,1)S(1)}, bf16[2,512,512]{2,1,0:T(8,128)(2,1)}, u32[]{:S(2)}) copy-start(bf16[2,512,512]{2,1,0:T(8,128)(2,1)} %get-tuple-element.62) | copy-start | bytes 3145732
  354.4 29.1 %collective-permute-start.8 = (bf16[72,512]{1,0:T(8,128)(2,1)S(1)}, bf16[72,512]{1,0:T(8,128)(2,1)S(1)}, u32[]{:S(2)}, u32[]{:S(2)}) collective-permute-start(bf16[72,512]{1,0:T(8,128)(2,1)S(1)} %fusion.13), channel_id=1, source_target_pairs={{0,16},{8,24},{16,0},{24,8},{1,17},{9,25},{17,1},{25,9},{2,18},{10... | collective-permute-start | bytes 221192 | tf_op jit(solution)/shard_map/ppermute | solution.py:335
  378.4 5.1 %collective-permute-start.7 = (bf16[72,512]{1,0:T(8,128)(2,1)S(1)}, bf16[72,512]{1,0:T(8,128)(2,1)S(1)}, u32[]{:S(2)}, u32[]{:S(2)}) collective-permute-start(bf16[72,512]{1,0:T(8,128)(2,1)S(1)} %fusion.13), channel_id=1, source_target_pairs={{0,8},{8,0},{16,24},{24,16},{1,9},{9,1},{17,25},{25,17},{2,10},{10... | collective-permute-start | bytes 221192 | tf_op jit(solution)/shard_map/ppermute | solution.py:335
  385.9 7.6 %collective-permute-start.14 = (bf16[200,512]{1,0:T(8,128)(2,1)S(1)}, bf16[200,512]{1,0:T(8,128)(2,1)S(1)}, u32[]{:S(2)}, u32[]{:S(2)}) collective-permute-start(bf16[200,512]{1,0:T(8,128)(2,1)S(1)} %get-tuple-element.107), channel_id=1, source_target_pairs={{0,2},{1,3},{2,0},{3,1},{4,6},{5,7},{6,4},{7,5},{8,10},{9,11},{10,... | collective-permute-start | bytes 614408 | tf_op jit(solution)/shard_map/ppermute | solution.py:334
  387.3 10.1 %collective-permute-start.16 = (bf16[200,512]{1,0:T(8,128)(2,1)S(1)}, bf16[200,512]{1,0:T(8,128)(2,1)S(1)}, u32[]{:S(2)}, u32[]{:S(2)}) collective-permute-start(bf16[200,512]{1,0:T(8,128)(2,1)S(1)} %get-tuple-element.108), channel_id=1, source_target_pairs={{0,6},{1,7},{2,4},{3,5},{4,2},{5,3},{6,0},{7,1},{8,14},{9,15},{10,... | collective-permute-start | bytes 614408 | tf_op jit(solution)/shard_map/ppermute | solution.py:334
  389.7 14.2 %collective-permute-start.15 = (bf16[200,512]{1,0:T(8,128)(2,1)S(1)}, bf16[200,512]{1,0:T(8,128)(2,1)S(1)}, u32[]{:S(2)}, u32[]{:S(2)}) collective-permute-start(bf16[200,512]{1,0:T(8,128)(2,1)S(1)} %get-tuple-element.109), channel_id=1, source_target_pairs={{0,4},{1,5},{2,6},{3,7},{4,0},{5,1},{6,2},{7,3},{8,12},{9,13},{10,... | collective-permute-start | bytes 614408 | tf_op jit(solution)/shard_map/ppermute | solution.py:334
  404.1 7.9 %collective-permute-start.19 = (bf16[200,512]{1,0:T(8,128)(2,1)S(1)}, bf16[200,512]{1,0:T(8,128)(2,1)S(1)}, u32[]{:S(2)}, u32[]{:S(2)}) collective-permute-start(bf16[200,512]{1,0:T(8,128)(2,1)S(1)} %fusion.10), channel_id=1, source_target_pairs={{0,24},{8,16},{16,8},{24,0},{1,25},{9,17},{17,9},{25,1},{2,26},{10... | collective-permute-start | bytes 614408 | tf_op jit(solution)/shard_map/ppermute | solution.py:335
  405.5 8.5 %collective-permute-start.18 = (bf16[200,512]{1,0:T(8,128)(2,1)S(1)}, bf16[200,512]{1,0:T(8,128)(2,1)S(1)}, u32[]{:S(2)}, u32[]{:S(2)}) collective-permute-start(bf16[200,512]{1,0:T(8,128)(2,1)S(1)} %fusion.10), channel_id=1, source_target_pairs={{0,16},{8,24},{16,0},{24,8},{1,17},{9,25},{17,1},{25,9},{2,18},{10... | collective-permute-start | bytes 614408 | tf_op jit(solution)/shard_map/ppermute | solution.py:335
  406.6 7.4 %collective-permute-start.17 = (bf16[200,512]{1,0:T(8,128)(2,1)S(1)}, bf16[200,512]{1,0:T(8,128)(2,1)S(1)}, u32[]{:S(2)}, u32[]{:S(2)}) collective-permute-start(bf16[200,512]{1,0:T(8,128)(2,1)S(1)} %fusion.10), channel_id=1, source_target_pairs={{0,8},{8,0},{16,24},{24,16},{1,9},{9,1},{17,25},{25,17},{2,10},{10... | collective-permute-start | bytes 614408 | tf_op jit(solution)/shard_map/ppermute | solution.py:335
  (1 other events, 0.7 us)
